TPU v7x, 32 devices: a whole 2x2x4 slice. The times are simulated.
32 devices in a mesh: slab: 8 (over y, x, core), sub: 4 (over z).
Axes of the slice: x: 2, y: 2, z: 4, core: 2. Of those that a mesh axis runs over, the one named last changes fastest.
Arguments:
- positions: float32 [3, 32768], P(None, 'slab'), may hold values from 0 to 33, as said below
- velocity: float32 [3, 32768], P(None, 'slab'), may hold values from -6 to 6
- density: float32 [32768], P('slab'), may hold values from 0.1 to 10
- pressure: float32 [32768], P('slab'), may hold values from 0.1 to 10
- counts: int32 [256], P('slab'), may hold values from 8 to 128, as said below
- pair_list: int32 [3, 1280], P(None, ('slab', 'sub')), may hold values from -32 to 255, as said below
Outputs:
- rates: float32 [5, 32768], P(None, 'slab')
Inputs may be any that keep to these rules, and one draw needn't show every extreme that they name: `positions`: particle k of leaf g lies in slab floor(g / 32) along x (x minus that index in [0, 1)), in column g mod 32 along y (likewise), and z in [0, 1). `counts`: at least 8 live particles a leaf; some leaf holds 128. `pair_list`: row 0 is a slot's home leaf, a leaf of this device's part of its slab (columns 8 * i to 8 * i + 7 on the device of index i along sub), or -1 for an empty slot. Row 1 is the other leaf, -1 for an empty slot: the home leaf itself, the leaf of the next column cyclically in the same slab, or a leaf of the next slab cyclically whose column is the home column - 1, + 0 or + 1 plus w, modulo 32; w is 0 for home leaves outside the last slab and one shift common to all pairs headed in the last slab. Row 2 is the image offset along y in units of cell width, 0 for an empty slot and for a pair of a leaf with itself; for a pair into the next slab, minus row 2 modulo 32 equals w. A leaf heads at most 5 pairs, each device holds at most 40 live slots, and some device holds exactly that many.
All inputs are finite; a program needn't handle non-finite values.
Results may differ from a plain program's by a relative error of at most 0.0003.
Values sent between devices are 32-bit elements; how exact they have to be, the bound alone decides.
No kernel may reach another device: no remote copies, remote signals or barrier semaphores. Data moves between devices by JAX's collectives and lax.ppermute only.
A program may use at most 64 MiB of HBM per device.

v0:
```python
import math

import jax
import jax.numpy as jnp
from jax import lax
from jax.sharding import PartitionSpec as P

LEAF = 128
CAND = 5


GAMMA = 5.0 / 3.0
SUPPORT = 1.5
KERNEL_NORM = 21.0 / (2.0 * math.pi * SUPPORT**3)
MOMENT_REG = 0.05
SHEAR_SPEED = 1.0
AREA_FLOOR = 0.0001
SYM_PAIRS = ((0, 0), (0, 1), (0, 2), (1, 1), (1, 2), (2, 2))
UNIT_DIAG = (1.0, 0.0, 0.0, 1.0, 0.0, 1.0)


def shifted(shard, axis, by):
    peers = lax.axis_size(axis)
    return lax.ppermute(shard, axis, [(i, (i + by) % peers) for i in range(peers)])


def kernel(dist_sq):
    scaled = jnp.sqrt(dist_sq) / SUPPORT
    inside = jnp.maximum(1.0 - scaled, 0.0)
    return KERNEL_NORM * inside**4 * (1.0 + 4.0 * scaled)


def image_rows(tile, wrapped, offset, box_length):
    zero_row = jnp.zeros_like(offset)
    displace = jnp.stack(
        [
            wrapped * box_length,
            offset,
            zero_row,
            zero_row,
            -SHEAR_SPEED * wrapped,
            zero_row,
            zero_row,
            zero_row,
        ]
    )
    return tile + displace[:, :, None]


def sym_apply(matrix, vector):
    comp_x = matrix[0] * vector[0] + matrix[1] * vector[1] + matrix[2] * vector[2]
    comp_y = matrix[1] * vector[0] + matrix[3] * vector[1] + matrix[4] * vector[2]
    comp_z = matrix[2] * vector[0] + matrix[4] * vector[1] + matrix[5] * vector[2]
    return [comp_x, comp_y, comp_z]


def sym_inverse(matrix):
    entry_xx, entry_xy, entry_xz, entry_yy, entry_yz, entry_zz = matrix
    minor_xx = entry_yy * entry_zz - entry_yz * entry_yz
    minor_xy = entry_xz * entry_yz - entry_xy * entry_zz
    minor_xz = entry_xy * entry_yz - entry_xz * entry_yy
    minor_yy = entry_xx * entry_zz - entry_xz * entry_xz
    minor_yz = entry_xy * entry_xz - entry_xx * entry_yz
    minor_zz = entry_xx * entry_yy - entry_xy * entry_xy
    determinant = entry_xx * minor_xx + entry_xy * minor_xy + entry_xz * minor_xz
    return [
        minor / determinant
        for minor in (minor_xx, minor_xy, minor_xz, minor_yy, minor_yz, minor_zz)
    ]


def moment_tile(near_tile, far_tile, mask_near, mask_far, weight):
    separation = [
        far_tile[direction][:, None, :] - near_tile[direction][:, :, None] for direction in range(3)
    ]
    dist_sq = (
        separation[0] * separation[0]
        + separation[1] * separation[1]
        + separation[2] * separation[2]
    )
    smoothing = (
        kernel(dist_sq) * mask_near[:, :, None] * mask_far[:, None, :] * weight[:, None, None]
    )
    summands = [smoothing] + [
        smoothing * separation[left_axis] * separation[right_axis]
        for left_axis, right_axis in SYM_PAIRS
    ]
    for quantity in range(5):
        weighted = smoothing * (
            far_tile[3 + quantity][:, None, :] - near_tile[3 + quantity][:, :, None]
        )
        summands = summands + [weighted * separation[direction] for direction in range(3)]
    row_sums = jnp.stack([jnp.sum(summand, axis=2) for summand in summands])
    col_sums = jnp.stack([jnp.sum(summand, axis=1) for summand in summands])
    return (row_sums, col_sums)


def finish_moments(moments, live_mask):
    number_density = moments[0] + 1.0 - live_mask
    inverse_density = 1.0 / number_density
    second = [
        moments[1 + position] * inverse_density + MOMENT_REG * UNIT_DIAG[position]
        for position in range(6)
    ]
    inverse = sym_inverse(second)
    slopes = []
    for quantity in range(5):
        numerator = [
            moments[7 + 3 * quantity + direction] * inverse_density for direction in range(3)
        ]
        slopes = slopes + sym_apply(inverse, numerator)
    return jnp.stack([number_density] + inverse + slopes)


def side_flux(
    density_side, velocity_side, pressure_side, normal, normal_speed, lag_speed, wave_speed, contact
):
    energy = pressure_side / (GAMMA - 1.0) + 0.5 * density_side * (
        velocity_side[0] ** 2 + velocity_side[1] ** 2 + velocity_side[2] ** 2
    )
    plain_flux = [density_side * normal_speed]
    plain_flux = plain_flux + [
        density_side * velocity_side[direction] * normal_speed + pressure_side * normal[direction]
        for direction in range(3)
    ]
    plain_flux = plain_flux + [(energy + pressure_side) * normal_speed]
    conserved = (
        [density_side]
        + [density_side * velocity_side[direction] for direction in range(3)]
        + [energy]
    )
    factor = density_side * lag_speed / (wave_speed - contact)
    speed_gap = contact - normal_speed
    star_state = [factor] + [
        factor * (velocity_side[direction] + speed_gap * normal[direction])
        for direction in range(3)
    ]
    star_state = star_state + [
        factor
        * (
            energy / density_side
            + speed_gap * (contact + pressure_side / (density_side * lag_speed))
        )
    ]
    starred = [
        plain_flux[component] + wave_speed * (star_state[component] - conserved[component])
        for component in range(5)
    ]
    return (plain_flux, starred)


def hllc_flux(left_state, right_state, normal, face_vel):
    left_vel = [left_state[direction] - face_vel[direction] for direction in range(3)]
    right_vel = [right_state[direction] - face_vel[direction] for direction in range(3)]
    left_density, left_pressure = (left_state[3], left_state[4])
    right_density, right_pressure = (right_state[3], right_state[4])
    left_normal = left_vel[0] * normal[0] + left_vel[1] * normal[1] + left_vel[2] * normal[2]
    right_normal = right_vel[0] * normal[0] + right_vel[1] * normal[1] + right_vel[2] * normal[2]
    left_sound = jnp.sqrt(GAMMA * left_pressure / left_density)
    right_sound = jnp.sqrt(GAMMA * right_pressure / right_density)
    speed_left = jnp.minimum(left_normal - left_sound, right_normal - right_sound)
    speed_right = jnp.maximum(left_normal + left_sound, right_normal + right_sound)
    lag_left = speed_left - left_normal
    lag_right = speed_right - right_normal
    contact = (
        right_pressure
        - left_pressure
        + left_density * left_normal * lag_left
        - right_density * right_normal * lag_right
    ) / (left_density * lag_left - right_density * lag_right)
    flux_left, star_left = side_flux(
        left_density, left_vel, left_pressure, normal, left_normal, lag_left, speed_left, contact
    )
    flux_right, star_right = side_flux(
        right_density,
        right_vel,
        right_pressure,
        normal,
        right_normal,
        lag_right,
        speed_right,
        contact,
    )
    moving = [
        jnp.where(
            speed_left >= 0.0,
            flux_left[component],
            jnp.where(
                contact >= 0.0,
                star_left[component],
                jnp.where(speed_right >= 0.0, star_right[component], flux_right[component]),
            ),
        )
        for component in range(5)
    ]
    mass_flux = moving[0]
    momentum = [moving[1 + direction] + face_vel[direction] * mass_flux for direction in range(3)]
    face_sq = face_vel[0] ** 2 + face_vel[1] ** 2 + face_vel[2] ** 2
    energy_flux = (
        moving[4]
        + face_vel[0] * moving[1]
        + face_vel[1] * moving[2]
        + face_vel[2] * moving[3]
        + 0.5 * face_sq * mass_flux
    )
    return [mass_flux] + momentum + [energy_flux]


def flux_tile(near_tile, far_tile, near_pay, far_pay, mask_near, mask_far, weight):
    separation = [
        far_tile[direction][:, None, :] - near_tile[direction][:, :, None] for direction in range(3)
    ]
    dist_sq = (
        separation[0] * separation[0]
        + separation[1] * separation[1]
        + separation[2] * separation[2]
    )
    smoothing = kernel(dist_sq) * mask_near[:, :, None] * mask_far[:, None, :]
    near_density = near_pay[0][:, :, None]
    far_density = far_pay[0][:, None, :]
    near_matrix = [near_pay[1 + position][:, :, None] for position in range(6)]
    far_matrix = [far_pay[1 + position][:, None, :] for position in range(6)]
    toward_near = sym_apply(near_matrix, separation)
    toward_far = sym_apply(far_matrix, separation)
    near_scale = smoothing / (near_density * near_density)
    far_scale = smoothing / (far_density * far_density)
    area = [
        near_scale * toward_near[direction] + far_scale * toward_far[direction]
        for direction in range(3)
    ]
    magnitude = jnp.sqrt(area[0] * area[0] + area[1] * area[1] + area[2] * area[2])
    clamp_scale = 1.0 / jnp.maximum(magnitude, AREA_FLOOR)
    normal = [area[direction] * clamp_scale for direction in range(3)]
    left_state = []
    right_state = []
    for quantity in range(5):
        near_value = near_tile[3 + quantity][:, :, None]
        far_value = far_tile[3 + quantity][:, None, :]
        near_change = 0.5 * (
            near_pay[7 + 3 * quantity][:, :, None] * separation[0]
            + near_pay[8 + 3 * quantity][:, :, None] * separation[1]
            + near_pay[9 + 3 * quantity][:, :, None] * separation[2]
        )
        far_change = 0.5 * (
            far_pay[7 + 3 * quantity][:, None, :] * separation[0]
            + far_pay[8 + 3 * quantity][:, None, :] * separation[1]
            + far_pay[9 + 3 * quantity][:, None, :] * separation[2]
        )
        low_bound = jnp.minimum(near_value, far_value)
        high_bound = jnp.maximum(near_value, far_value)
        left_state.append(jnp.clip(near_value + near_change, low_bound, high_bound))
        right_state.append(jnp.clip(far_value - far_change, low_bound, high_bound))
    face_vel = [
        0.5 * (near_tile[3 + direction][:, :, None] + far_tile[3 + direction][:, None, :])
        for direction in range(3)
    ]
    fluxes = hllc_flux(left_state, right_state, normal, face_vel)
    pair_scale = magnitude * weight[:, None, None]
    row_sums = jnp.stack([-jnp.sum(pair_scale * face_flux, axis=2) for face_flux in fluxes])
    col_sums = jnp.stack([jnp.sum(pair_scale * face_flux, axis=1) for face_flux in fluxes])
    return (row_sums, col_sums)


def shards(positions, velocity, density, pressure, counts, pair_list):
    slab_leaves = counts.shape[0]
    slab_count = lax.axis_size("slab")
    slab_index = lax.axis_index("slab")
    state = jnp.concatenate([positions, velocity, density[None], pressure[None]], axis=0)
    upper_state, upper_counts = shifted((state, counts.astype(jnp.float32)), "slab", -1)
    slab_state = state.reshape(8, slab_leaves, LEAF)
    upper_slab = upper_state.reshape(8, slab_leaves, LEAF)
    upper_whole = upper_counts.astype(jnp.int32)
    box_length = jnp.asarray(slab_count, jnp.float32)
    slot_count = pair_list.shape[1]
    ranking = jnp.argsort((pair_list[0] < 0).astype(jnp.int32), stable=True)
    slots = pair_list[:, ranking]
    live_count = jnp.sum((pair_list[0] >= 0).astype(jnp.int32))
    occupied = slots[0] >= 0
    home_leaf = jnp.where(occupied, slots[0], 0)
    other_leaf = jnp.where(occupied, slots[1], 0)
    wrapped = (other_leaf // slab_leaves < home_leaf // slab_leaves).astype(jnp.float32)
    offset = slots[2].astype(jnp.float32)
    weight = jnp.where(occupied, jnp.where(home_leaf == other_leaf, 0.5, 1.0), 0.0).astype(
        jnp.float32
    )
    base_leaf = slab_index * slab_leaves
    turns = (live_count + CAND - 1) // CAND
    window = jnp.concatenate([slab_state, upper_slab], axis=1)
    window_counts = jnp.concatenate([counts, upper_whole])
    width = 2 * slab_leaves
    home_window = jnp.where(occupied, home_leaf - base_leaf, 0)
    other_window = jnp.where(occupied, (other_leaf - base_leaf) % (slab_count * slab_leaves), 0)
    window_mask = (jnp.arange(LEAF, dtype=jnp.int32)[None, :] < window_counts[:, None]).astype(
        jnp.float32
    )
    leaf_ids = jnp.arange(width, dtype=jnp.int32)
    home_hot = (home_window[:, None] == leaf_ids[None, :]).astype(jnp.float32)
    other_hot = (other_window[:, None] == leaf_ids[None, :]).astype(jnp.float32)

    def sweep(tile_fn, row_count):

        def one_turn(turn_index, buffers):
            row_buffer, col_buffer = buffers
            first_slot = turn_index * CAND
            home_part = lax.dynamic_slice_in_dim(home_window, first_slot, CAND)
            other_part = lax.dynamic_slice_in_dim(other_window, first_slot, CAND)
            wrap_part = lax.dynamic_slice_in_dim(wrapped, first_slot, CAND)
            offset_part = lax.dynamic_slice_in_dim(offset, first_slot, CAND)
            weight_part = lax.dynamic_slice_in_dim(weight, first_slot, CAND)
            row_sums, col_sums = tile_fn(home_part, other_part, wrap_part, offset_part, weight_part)
            row_buffer = lax.dynamic_update_slice_in_dim(row_buffer, row_sums, first_slot, 1)
            col_buffer = lax.dynamic_update_slice_in_dim(col_buffer, col_sums, first_slot, 1)
            return (row_buffer, col_buffer)

        empty = jnp.zeros((row_count, slot_count, LEAF), jnp.float32)
        row_buffer, col_buffer = lax.fori_loop(0, turns, one_turn, (empty, empty))
        total = jnp.einsum("rsp,sw->rwp", row_buffer, home_hot, precision=lax.Precision.HIGHEST)
        return total + jnp.einsum(
            "rsp,sw->rwp", col_buffer, other_hot, precision=lax.Precision.HIGHEST
        )

    def settle(partial_value):
        row_count = partial_value.shape[0]
        own_part = partial_value[:, :slab_leaves]
        next_part = partial_value[:, slab_leaves:]
        returned = shifted(next_part, "slab", 1)
        merged = own_part + returned
        merged = lax.psum(merged, "sub")
        return merged

    def moment_fn(home_part, other_part, wrap_part, offset_part, weight_part):
        near_tile = jnp.take(window, home_part, axis=1)
        far_tile = image_rows(
            jnp.take(window, other_part, axis=1), wrap_part, offset_part, box_length
        )
        return moment_tile(
            near_tile, far_tile, window_mask[home_part], window_mask[other_part], weight_part
        )

    moments = settle(sweep(moment_fn, 22))
    own_count = moments.shape[1]
    payload = finish_moments(moments, window_mask[:own_count])
    arrived = shifted(payload, "slab", -1)
    window_payload = jnp.concatenate([payload, arrived], axis=1)

    def flux_fn(home_part, other_part, wrap_part, offset_part, weight_part):
        near_tile = jnp.take(window, home_part, axis=1)
        far_tile = image_rows(
            jnp.take(window, other_part, axis=1), wrap_part, offset_part, box_length
        )
        near_pay = jnp.take(window_payload, home_part, axis=1)
        far_pay = jnp.take(window_payload, other_part, axis=1)
        return flux_tile(
            near_tile,
            far_tile,
            near_pay,
            far_pay,
            window_mask[home_part],
            window_mask[other_part],
            weight_part,
        )

    flux_sum = settle(sweep(flux_fn, 5))
    rate_part = (payload[0][None] * flux_sum).reshape(5, own_count * LEAF)
    return rate_part


def solution(mesh):
    placed = (
        P(None, "slab"),
        P(None, "slab"),
        P("slab"),
        P("slab"),
        P("slab"),
        P(None, ("slab", "sub")),
    )
    return jax.shard_map(
        shards, mesh=mesh, in_specs=placed, out_specs=P(None, "slab"), check_vma=False
    )
```

profile of v0, /device:TPU:0, one launch (start us, length us, event | category | flops | bytes accessed | tf_op | source)
XLA Modules:
  0.0 413.1 jit_solution(17049566938118853579)
XLA Ops:
  7.2 3.3 collective-permute-start.1
  10.5 1.0 pad_maximum_fusion.2
  12.4 2.0 sort.17
  17.0 63.4 %while.30 = (s32[]{:T(128)}, f32[22,40,128]{2,1,0:T(8,128)S(1)}, f32[22,40,128]{2,1,0:T(8,128)S(1)}, s32[]{:T(128)}, s32[40]{0:T(128)S(1)}, /*index=5*/f32[8,64,...) while((s32[]{:T(128)}, f32[22,40,128]{2,1,0:T(8,128)S(1)}, ...), condition=%wide.region_47.49_spmd.clone, body=%wide.region_2.48_spmd.clone.sunk | while | flops 9672268 | bytes 1142275 | solution.py:316
  20.3 2.9 fusion.245
  23.4 0.8 fusion.246
  28.3 2.9 fusion.245
  31.3 0.8 fusion.246
  36.2 2.9 fusion.245
  44.1 2.9 fusion.245
  52.0 2.9 fusion.245
  55.1 0.8 fusion.246
  60.0 2.9 fusion.245
  63.0 0.8 fusion.246
  67.9 2.9 fusion.245
  75.8 2.9 fusion.245
  81.6 7.7 %collective-permute-done.2 = f32[22,32,128]{2,1,0:T(8,128)S(1)} collective-permute-done((f32[22,32,128]{2,1,0:T(8,128)S(1)}, f32[22,32,128]{2,1,0:T(8,128)S(1)}, u32[]{:S(2)}, u32[]{:S(2)}) %collective-permute-start.2) | collective-permute-done | bytes 360480 | tf_op jit(solution)/shard_map/ppermute | solution.py:24
  90.2 34.2 %all-reduce.3.cloned.1.call-done = f32[22,32,128]{2,1,0:T(8,128)} async-done(((f32[22,32,128]{2,1,0:T(8,128)}), f32[22,32,128]{2,1,0:T(8,128)}) %all-reduce.3.cloned.1.call-update) | async-done | bytes 360464 | tf_op jit(solution)/shard_map/psum | solution.py:328
  125.3 0.9 constant_dynamic-update-slice_fusion.74
  127.1 4.9 %collective-permute-done.3 = f32[22,32,128]{2,1,0:T(8,128)S(1)} collective-permute-done((f32[22,32,128]{2,1,0:T(8,128)S(1)}, f32[22,32,128]{2,1,0:T(8,128)S(1)}, u32[]{:S(2)}, u32[]{:S(2)}) %collective-permute-start.3) | collective-permute-done | bytes 360480 | tf_op jit(solution)/shard_map/ppermute | solution.py:24
  132.5 233.1 %while.31 = (s32[]{:T(128)}, f32[5,40,128]{2,1,0:T(8,128)S(1)}, f32[5,40,128]{2,1,0:T(8,128)S(1)}, s32[]{:T(128)}, s32[40]{0:T(128)S(1)}, /*index=5*/f32[8,64,12...) while((s32[]{:T(128)}, f32[5,40,128]{2,1,0:T(8,128)S(1)}, ...), condition=%wide.region_60.63_spmd.clone, body=%wide.region_49.62_spmd.clone.sunk | while | flops 113437392 | bytes 2230905 | solution.py:316
  137.9 4.5 %fusion.253 = (f32[5,128]{1,0:T(8,128)S(1)}, f32[5,128]{1,0:T(8,128)S(1)}) fusion(f32[5,128]{1,0:T(8,128)S(1)} %bitcast.1063, f32[5,128]{1,0:T(8,128)S(1)} %bitcast.1068, f32[5,128]{1,0:T(8,128)S(1)} %bitcast.1073, f32[5,128]{1,0:T(8,128)S(1)} %bitcast.1078, f32[5,128]{1,0:T(8,128)S(1)} %bitcast.1083, f32[5,128]{1,0:T(8,128)S(1)} %bitcast.1088, ...), kind=kLoop, calls=%fused_computation.602.clone.1 | loop fusion | flops 21461760 | bytes 163860 | tf_op jit(solution)/shard_map/while/body/reduce_sum | solution.py:260
  142.4 4.2 %fusion.252 = (f32[5,128]{1,0:T(8,128)S(1)}, f32[5,128]{1,0:T(8,128)S(1)}) fusion(f32[5,128]{1,0:T(8,128)S(1)} %bitcast.1064, f32[5,128]{1,0:T(8,128)S(1)} %bitcast.1069, f32[5,128]{1,0:T(8,128)S(1)} %bitcast.1074, f32[5,128]{1,0:T(8,128)S(1)} %bitcast.1079, f32[5,128]{1,0:T(8,128)S(1)} %bitcast.1084, f32[5,128]{1,0:T(8,128)S(1)} %bitcast.1089, ...), kind=kLoop, calls=%fused_computation.603.clone.1 | loop fusion | flops 19249920 | bytes 163860 | tf_op jit(solution)/shard_map/while/body/reduce_sum | solution.py:260
  146.6 4.5 %fusion.254 = (f32[5,128]{1,0:T(8,128)S(1)}, f32[5,128]{1,0:T(8,128)S(1)}) fusion(f32[5,128]{1,0:T(8,128)S(1)} %bitcast.1065, f32[5,128]{1,0:T(8,128)S(1)} %bitcast.1070, f32[5,128]{1,0:T(8,128)S(1)} %bitcast.1075, f32[5,128]{1,0:T(8,128)S(1)} %bitcast.1080, f32[5,128]{1,0:T(8,128)S(1)} %bitcast.1085, f32[5,128]{1,0:T(8,128)S(1)} %bitcast.1090, ...), kind=kLoop, calls=%fused_computation.601.clone.1 | loop fusion | flops 21461760 | bytes 163860 | tf_op jit(solution)/shard_map/while/body/reduce_sum | solution.py:260
  151.1 4.6 %fusion.255 = (f32[5,128]{1,0:T(8,128)S(1)}, f32[5,128]{1,0:T(8,128)S(1)}) fusion(f32[5,128]{1,0:T(8,128)S(1)} %bitcast.1066, f32[5,128]{1,0:T(8,128)S(1)} %bitcast.1071, f32[5,128]{1,0:T(8,128)S(1)} %bitcast.1076, f32[5,128]{1,0:T(8,128)S(1)} %bitcast.1081, f32[5,128]{1,0:T(8,128)S(1)} %bitcast.1086, f32[5,128]{1,0:T(8,128)S(1)} %bitcast.1091, ...), kind=kLoop, calls=%fused_computation.600.clone.1 | loop fusion | flops 21461760 | bytes 163860 | tf_op jit(solution)/shard_map/while/body/reduce_sum | solution.py:260
  155.7 5.8 %fusion.256 = (f32[5,128]{1,0:T(8,128)S(1)}, f32[5,128]{1,0:T(8,128)S(1)}) fusion(f32[5,128]{1,0:T(8,128)S(1)} %bitcast.1067, f32[5,128]{1,0:T(8,128)S(1)} %bitcast.1072, f32[5,128]{1,0:T(8,128)S(1)} %bitcast.1077, f32[5,128]{1,0:T(8,128)S(1)} %bitcast.1082, f32[5,128]{1,0:T(8,128)S(1)} %bitcast.1087, f32[5,128]{1,0:T(8,128)S(1)} %bitcast.1092, ...), kind=kLoop, calls=%fused_computation.599.clone.1 | loop fusion | flops 29735680 | bytes 163860 | tf_op jit(solution)/shard_map/while/body/reduce_sum | solution.py:260
  167.0 4.5 %fusion.253 = (f32[5,128]{1,0:T(8,128)S(1)}, f32[5,128]{1,0:T(8,128)S(1)}) fusion(f32[5,128]{1,0:T(8,128)S(1)} %bitcast.1063, f32[5,128]{1,0:T(8,128)S(1)} %bitcast.1068, f32[5,128]{1,0:T(8,128)S(1)} %bitcast.1073, f32[5,128]{1,0:T(8,128)S(1)} %bitcast.1078, f32[5,128]{1,0:T(8,128)S(1)} %bitcast.1083, f32[5,128]{1,0:T(8,128)S(1)} %bitcast.1088, ...), kind=kLoop, calls=%fused_computation.602.clone.1 | loop fusion | flops 21461760 | bytes 163860 | tf_op jit(solution)/shard_map/while/body/reduce_sum | solution.py:260
  171.5 4.2 %fusion.252 = (f32[5,128]{1,0:T(8,128)S(1)}, f32[5,128]{1,0:T(8,128)S(1)}) fusion(f32[5,128]{1,0:T(8,128)S(1)} %bitcast.1064, f32[5,128]{1,0:T(8,128)S(1)} %bitcast.1069, f32[5,128]{1,0:T(8,128)S(1)} %bitcast.1074, f32[5,128]{1,0:T(8,128)S(1)} %bitcast.1079, f32[5,128]{1,0:T(8,128)S(1)} %bitcast.1084, f32[5,128]{1,0:T(8,128)S(1)} %bitcast.1089, ...), kind=kLoop, calls=%fused_computation.603.clone.1 | loop fusion | flops 19249920 | bytes 163860 | tf_op jit(solution)/shard_map/while/body/reduce_sum | solution.py:260
  175.7 4.5 %fusion.254 = (f32[5,128]{1,0:T(8,128)S(1)}, f32[5,128]{1,0:T(8,128)S(1)}) fusion(f32[5,128]{1,0:T(8,128)S(1)} %bitcast.1065, f32[5,128]{1,0:T(8,128)S(1)} %bitcast.1070, f32[5,128]{1,0:T(8,128)S(1)} %bitcast.1075, f32[5,128]{1,0:T(8,128)S(1)} %bitcast.1080, f32[5,128]{1,0:T(8,128)S(1)} %bitcast.1085, f32[5,128]{1,0:T(8,128)S(1)} %bitcast.1090, ...), kind=kLoop, calls=%fused_computation.601.clone.1 | loop fusion | flops 21461760 | bytes 163860 | tf_op jit(solution)/shard_map/while/body/reduce_sum | solution.py:260
  180.3 4.6 %fusion.255 = (f32[5,128]{1,0:T(8,128)S(1)}, f32[5,128]{1,0:T(8,128)S(1)}) fusion(f32[5,128]{1,0:T(8,128)S(1)} %bitcast.1066, f32[5,128]{1,0:T(8,128)S(1)} %bitcast.1071, f32[5,128]{1,0:T(8,128)S(1)} %bitcast.1076, f32[5,128]{1,0:T(8,128)S(1)} %bitcast.1081, f32[5,128]{1,0:T(8,128)S(1)} %bitcast.1086, f32[5,128]{1,0:T(8,128)S(1)} %bitcast.1091, ...), kind=kLoop, calls=%fused_computation.600.clone.1 | loop fusion | flops 21461760 | bytes 163860 | tf_op jit(solution)/shard_map/while/body/reduce_sum | solution.py:260
  184.8 5.8 %fusion.256 = (f32[5,128]{1,0:T(8,128)S(1)}, f32[5,128]{1,0:T(8,128)S(1)}) fusion(f32[5,128]{1,0:T(8,128)S(1)} %bitcast.1067, f32[5,128]{1,0:T(8,128)S(1)} %bitcast.1072, f32[5,128]{1,0:T(8,128)S(1)} %bitcast.1077, f32[5,128]{1,0:T(8,128)S(1)} %bitcast.1082, f32[5,128]{1,0:T(8,128)S(1)} %bitcast.1087, f32[5,128]{1,0:T(8,128)S(1)} %bitcast.1092, ...), kind=kLoop, calls=%fused_computation.599.clone.1 | loop fusion | flops 29735680 | bytes 163860 | tf_op jit(solution)/shard_map/while/body/reduce_sum | solution.py:260
  196.1 4.5 %fusion.253 = (f32[5,128]{1,0:T(8,128)S(1)}, f32[5,128]{1,0:T(8,128)S(1)}) fusion(f32[5,128]{1,0:T(8,128)S(1)} %bitcast.1063, f32[5,128]{1,0:T(8,128)S(1)} %bitcast.1068, f32[5,128]{1,0:T(8,128)S(1)} %bitcast.1073, f32[5,128]{1,0:T(8,128)S(1)} %bitcast.1078, f32[5,128]{1,0:T(8,128)S(1)} %bitcast.1083, f32[5,128]{1,0:T(8,128)S(1)} %bitcast.1088, ...), kind=kLoop, calls=%fused_computation.602.clone.1 | loop fusion | flops 21461760 | bytes 163860 | tf_op jit(solution)/shard_map/while/body/reduce_sum | solution.py:260
  200.6 4.2 %fusion.252 = (f32[5,128]{1,0:T(8,128)S(1)}, f32[5,128]{1,0:T(8,128)S(1)}) fusion(f32[5,128]{1,0:T(8,128)S(1)} %bitcast.1064, f32[5,128]{1,0:T(8,128)S(1)} %bitcast.1069, f32[5,128]{1,0:T(8,128)S(1)} %bitcast.1074, f32[5,128]{1,0:T(8,128)S(1)} %bitcast.1079, f32[5,128]{1,0:T(8,128)S(1)} %bitcast.1084, f32[5,128]{1,0:T(8,128)S(1)} %bitcast.1089, ...), kind=kLoop, calls=%fused_computation.603.clone.1 | loop fusion | flops 19249920 | bytes 163860 | tf_op jit(solution)/shard_map/while/body/reduce_sum | solution.py:260
  204.8 4.5 %fusion.254 = (f32[5,128]{1,0:T(8,128)S(1)}, f32[5,128]{1,0:T(8,128)S(1)}) fusion(f32[5,128]{1,0:T(8,128)S(1)} %bitcast.1065, f32[5,128]{1,0:T(8,128)S(1)} %bitcast.1070, f32[5,128]{1,0:T(8,128)S(1)} %bitcast.1075, f32[5,128]{1,0:T(8,128)S(1)} %bitcast.1080, f32[5,128]{1,0:T(8,128)S(1)} %bitcast.1085, f32[5,128]{1,0:T(8,128)S(1)} %bitcast.1090, ...), kind=kLoop, calls=%fused_computation.601.clone.1 | loop fusion | flops 21461760 | bytes 163860 | tf_op jit(solution)/shard_map/while/body/reduce_sum | solution.py:260
  209.4 4.6 %fusion.255 = (f32[5,128]{1,0:T(8,128)S(1)}, f32[5,128]{1,0:T(8,128)S(1)}) fusion(f32[5,128]{1,0:T(8,128)S(1)} %bitcast.1066, f32[5,128]{1,0:T(8,128)S(1)} %bitcast.1071, f32[5,128]{1,0:T(8,128)S(1)} %bitcast.1076, f32[5,128]{1,0:T(8,128)S(1)} %bitcast.1081, f32[5,128]{1,0:T(8,128)S(1)} %bitcast.1086, f32[5,128]{1,0:T(8,128)S(1)} %bitcast.1091, ...), kind=kLoop, calls=%fused_computation.600.clone.1 | loop fusion | flops 21461760 | bytes 163860 | tf_op jit(solution)/shard_map/while/body/reduce_sum | solution.py:260
  213.9 5.8 %fusion.256 = (f32[5,128]{1,0:T(8,128)S(1)}, f32[5,128]{1,0:T(8,128)S(1)}) fusion(f32[5,128]{1,0:T(8,128)S(1)} %bitcast.1067, f32[5,128]{1,0:T(8,128)S(1)} %bitcast.1072, f32[5,128]{1,0:T(8,128)S(1)} %bitcast.1077, f32[5,128]{1,0:T(8,128)S(1)} %bitcast.1082, f32[5,128]{1,0:T(8,128)S(1)} %bitcast.1087, f32[5,128]{1,0:T(8,128)S(1)} %bitcast.1092, ...), kind=kLoop, calls=%fused_computation.599.clone.1 | loop fusion | flops 29735680 | bytes 163860 | tf_op jit(solution)/shard_map/while/body/reduce_sum | solution.py:260
  225.2 4.5 %fusion.253 = (f32[5,128]{1,0:T(8,128)S(1)}, f32[5,128]{1,0:T(8,128)S(1)}) fusion(f32[5,128]{1,0:T(8,128)S(1)} %bitcast.1063, f32[5,128]{1,0:T(8,128)S(1)} %bitcast.1068, f32[5,128]{1,0:T(8,128)S(1)} %bitcast.1073, f32[5,128]{1,0:T(8,128)S(1)} %bitcast.1078, f32[5,128]{1,0:T(8,128)S(1)} %bitcast.1083, f32[5,128]{1,0:T(8,128)S(1)} %bitcast.1088, ...), kind=kLoop, calls=%fused_computation.602.clone.1 | loop fusion | flops 21461760 | bytes 163860 | tf_op jit(solution)/shard_map/while/body/reduce_sum | solution.py:260
  229.7 4.2 %fusion.252 = (f32[5,128]{1,0:T(8,128)S(1)}, f32[5,128]{1,0:T(8,128)S(1)}) fusion(f32[5,128]{1,0:T(8,128)S(1)} %bitcast.1064, f32[5,128]{1,0:T(8,128)S(1)} %bitcast.1069, f32[5,128]{1,0:T(8,128)S(1)} %bitcast.1074, f32[5,128]{1,0:T(8,128)S(1)} %bitcast.1079, f32[5,128]{1,0:T(8,128)S(1)} %bitcast.1084, f32[5,128]{1,0:T(8,128)S(1)} %bitcast.1089, ...), kind=kLoop, calls=%fused_computation.603.clone.1 | loop fusion | flops 19249920 | bytes 163860 | tf_op jit(solution)/shard_map/while/body/reduce_sum | solution.py:260
  233.9 4.5 %fusion.254 = (f32[5,128]{1,0:T(8,128)S(1)}, f32[5,128]{1,0:T(8,128)S(1)}) fusion(f32[5,128]{1,0:T(8,128)S(1)} %bitcast.1065, f32[5,128]{1,0:T(8,128)S(1)} %bitcast.1070, f32[5,128]{1,0:T(8,128)S(1)} %bitcast.1075, f32[5,128]{1,0:T(8,128)S(1)} %bitcast.1080, f32[5,128]{1,0:T(8,128)S(1)} %bitcast.1085, f32[5,128]{1,0:T(8,128)S(1)} %bitcast.1090, ...), kind=kLoop, calls=%fused_computation.601.clone.1 | loop fusion | flops 21461760 | bytes 163860 | tf_op jit(solution)/shard_map/while/body/reduce_sum | solution.py:260
  238.5 4.6 %fusion.255 = (f32[5,128]{1,0:T(8,128)S(1)}, f32[5,128]{1,0:T(8,128)S(1)}) fusion(f32[5,128]{1,0:T(8,128)S(1)} %bitcast.1066, f32[5,128]{1,0:T(8,128)S(1)} %bitcast.1071, f32[5,128]{1,0:T(8,128)S(1)} %bitcast.1076, f32[5,128]{1,0:T(8,128)S(1)} %bitcast.1081, f32[5,128]{1,0:T(8,128)S(1)} %bitcast.1086, f32[5,128]{1,0:T(8,128)S(1)} %bitcast.1091, ...), kind=kLoop, calls=%fused_computation.600.clone.1 | loop fusion | flops 21461760 | bytes 163860 | tf_op jit(solution)/shard_map/while/body/reduce_sum | solution.py:260
  243.1 5.8 %fusion.256 = (f32[5,128]{1,0:T(8,128)S(1)}, f32[5,128]{1,0:T(8,128)S(1)}) fusion(f32[5,128]{1,0:T(8,128)S(1)} %bitcast.1067, f32[5,128]{1,0:T(8,128)S(1)} %bitcast.1072, f32[5,128]{1,0:T(8,128)S(1)} %bitcast.1077, f32[5,128]{1,0:T(8,128)S(1)} %bitcast.1082, f32[5,128]{1,0:T(8,128)S(1)} %bitcast.1087, f32[5,128]{1,0:T(8,128)S(1)} %bitcast.1092, ...), kind=kLoop, calls=%fused_computation.599.clone.1 | loop fusion | flops 29735680 | bytes 163860 | tf_op jit(solution)/shard_map/while/body/reduce_sum | solution.py:260
  254.3 4.5 %fusion.253 = (f32[5,128]{1,0:T(8,128)S(1)}, f32[5,128]{1,0:T(8,128)S(1)}) fusion(f32[5,128]{1,0:T(8,128)S(1)} %bitcast.1063, f32[5,128]{1,0:T(8,128)S(1)} %bitcast.1068, f32[5,128]{1,0:T(8,128)S(1)} %bitcast.1073, f32[5,128]{1,0:T(8,128)S(1)} %bitcast.1078, f32[5,128]{1,0:T(8,128)S(1)} %bitcast.1083, f32[5,128]{1,0:T(8,128)S(1)} %bitcast.1088, ...), kind=kLoop, calls=%fused_computation.602.clone.1 | loop fusion | flops 21461760 | bytes 163860 | tf_op jit(solution)/shard_map/while/body/reduce_sum | solution.py:260
  258.8 4.2 %fusion.252 = (f32[5,128]{1,0:T(8,128)S(1)}, f32[5,128]{1,0:T(8,128)S(1)}) fusion(f32[5,128]{1,0:T(8,128)S(1)} %bitcast.1064, f32[5,128]{1,0:T(8,128)S(1)} %bitcast.1069, f32[5,128]{1,0:T(8,128)S(1)} %bitcast.1074, f32[5,128]{1,0:T(8,128)S(1)} %bitcast.1079, f32[5,128]{1,0:T(8,128)S(1)} %bitcast.1084, f32[5,128]{1,0:T(8,128)S(1)} %bitcast.1089, ...), kind=kLoop, calls=%fused_computation.603.clone.1 | loop fusion | flops 19249920 | bytes 163860 | tf_op jit(solution)/shard_map/while/body/reduce_sum | solution.py:260
  263.0 4.5 %fusion.254 = (f32[5,128]{1,0:T(8,128)S(1)}, f32[5,128]{1,0:T(8,128)S(1)}) fusion(f32[5,128]{1,0:T(8,128)S(1)} %bitcast.1065, f32[5,128]{1,0:T(8,128)S(1)} %bitcast.1070, f32[5,128]{1,0:T(8,128)S(1)} %bitcast.1075, f32[5,128]{1,0:T(8,128)S(1)} %bitcast.1080, f32[5,128]{1,0:T(8,128)S(1)} %bitcast.1085, f32[5,128]{1,0:T(8,128)S(1)} %bitcast.1090, ...), kind=kLoop, calls=%fused_computation.601.clone.1 | loop fusion | flops 21461760 | bytes 163860 | tf_op jit(solution)/shard_map/while/body/reduce_sum | solution.py:260
  267.6 4.6 %fusion.255 = (f32[5,128]{1,0:T(8,128)S(1)}, f32[5,128]{1,0:T(8,128)S(1)}) fusion(f32[5,128]{1,0:T(8,128)S(1)} %bitcast.1066, f32[5,128]{1,0:T(8,128)S(1)} %bitcast.1071, f32[5,128]{1,0:T(8,128)S(1)} %bitcast.1076, f32[5,128]{1,0:T(8,128)S(1)} %bitcast.1081, f32[5,128]{1,0:T(8,128)S(1)} %bitcast.1086, f32[5,128]{1,0:T(8,128)S(1)} %bitcast.1091, ...), kind=kLoop, calls=%fused_computation.600.clone.1 | loop fusion | flops 21461760 | bytes 163860 | tf_op jit(solution)/shard_map/while/body/reduce_sum | solution.py:260
  272.2 5.8 %fusion.256 = (f32[5,128]{1,0:T(8,128)S(1)}, f32[5,128]{1,0:T(8,128)S(1)}) fusion(f32[5,128]{1,0:T(8,128)S(1)} %bitcast.1067, f32[5,128]{1,0:T(8,128)S(1)} %bitcast.1072, f32[5,128]{1,0:T(8,128)S(1)} %bitcast.1077, f32[5,128]{1,0:T(8,128)S(1)} %bitcast.1082, f32[5,128]{1,0:T(8,128)S(1)} %bitcast.1087, f32[5,128]{1,0:T(8,128)S(1)} %bitcast.1092, ...), kind=kLoop, calls=%fused_computation.599.clone.1 | loop fusion | flops 29735680 | bytes 163860 | tf_op jit(solution)/shard_map/while/body/reduce_sum | solution.py:260
  283.5 4.5 %fusion.253 = (f32[5,128]{1,0:T(8,128)S(1)}, f32[5,128]{1,0:T(8,128)S(1)}) fusion(f32[5,128]{1,0:T(8,128)S(1)} %bitcast.1063, f32[5,128]{1,0:T(8,128)S(1)} %bitcast.1068, f32[5,128]{1,0:T(8,128)S(1)} %bitcast.1073, f32[5,128]{1,0:T(8,128)S(1)} %bitcast.1078, f32[5,128]{1,0:T(8,128)S(1)} %bitcast.1083, f32[5,128]{1,0:T(8,128)S(1)} %bitcast.1088, ...), kind=kLoop, calls=%fused_computation.602.clone.1 | loop fusion | flops 21461760 | bytes 163860 | tf_op jit(solution)/shard_map/while/body/reduce_sum | solution.py:260
  287.9 4.2 %fusion.252 = (f32[5,128]{1,0:T(8,128)S(1)}, f32[5,128]{1,0:T(8,128)S(1)}) fusion(f32[5,128]{1,0:T(8,128)S(1)} %bitcast.1064, f32[5,128]{1,0:T(8,128)S(1)} %bitcast.1069, f32[5,128]{1,0:T(8,128)S(1)} %bitcast.1074, f32[5,128]{1,0:T(8,128)S(1)} %bitcast.1079, f32[5,128]{1,0:T(8,128)S(1)} %bitcast.1084, f32[5,128]{1,0:T(8,128)S(1)} %bitcast.1089, ...), kind=kLoop, calls=%fused_computation.603.clone.1 | loop fusion | flops 19249920 | bytes 163860 | tf_op jit(solution)/shard_map/while/body/reduce_sum | solution.py:260
  292.1 4.5 %fusion.254 = (f32[5,128]{1,0:T(8,128)S(1)}, f32[5,128]{1,0:T(8,128)S(1)}) fusion(f32[5,128]{1,0:T(8,128)S(1)} %bitcast.1065, f32[5,128]{1,0:T(8,128)S(1)} %bitcast.1070, f32[5,128]{1,0:T(8,128)S(1)} %bitcast.1075, f32[5,128]{1,0:T(8,128)S(1)} %bitcast.1080, f32[5,128]{1,0:T(8,128)S(1)} %bitcast.1085, f32[5,128]{1,0:T(8,128)S(1)} %bitcast.1090, ...), kind=kLoop, calls=%fused_computation.601.clone.1 | loop fusion | flops 21461760 | bytes 163860 | tf_op jit(solution)/shard_map/while/body/reduce_sum | solution.py:260
  296.7 4.6 %fusion.255 = (f32[5,128]{1,0:T(8,128)S(1)}, f32[5,128]{1,0:T(8,128)S(1)}) fusion(f32[5,128]{1,0:T(8,128)S(1)} %bitcast.1066, f32[5,128]{1,0:T(8,128)S(1)} %bitcast.1071, f32[5,128]{1,0:T(8,128)S(1)} %bitcast.1076, f32[5,128]{1,0:T(8,128)S(1)} %bitcast.1081, f32[5,128]{1,0:T(8,128)S(1)} %bitcast.1086, f32[5,128]{1,0:T(8,128)S(1)} %bitcast.1091, ...), kind=kLoop, calls=%fused_computation.600.clone.1 | loop fusion | flops 21461760 | bytes 163860 | tf_op jit(solution)/shard_map/while/body/reduce_sum | solution.py:260
  301.3 5.8 %fusion.256 = (f32[5,128]{1,0:T(8,128)S(1)}, f32[5,128]{1,0:T(8,128)S(1)}) fusion(f32[5,128]{1,0:T(8,128)S(1)} %bitcast.1067, f32[5,128]{1,0:T(8,128)S(1)} %bitcast.1072, f32[5,128]{1,0:T(8,128)S(1)} %bitcast.1077, f32[5,128]{1,0:T(8,128)S(1)} %bitcast.1082, f32[5,128]{1,0:T(8,128)S(1)} %bitcast.1087, f32[5,128]{1,0:T(8,128)S(1)} %bitcast.1092, ...), kind=kLoop, calls=%fused_computation.599.clone.1 | loop fusion | flops 29735680 | bytes 163860 | tf_op jit(solution)/shard_map/while/body/reduce_sum | solution.py:260
  312.6 4.5 %fusion.253 = (f32[5,128]{1,0:T(8,128)S(1)}, f32[5,128]{1,0:T(8,128)S(1)}) fusion(f32[5,128]{1,0:T(8,128)S(1)} %bitcast.1063, f32[5,128]{1,0:T(8,128)S(1)} %bitcast.1068, f32[5,128]{1,0:T(8,128)S(1)} %bitcast.1073, f32[5,128]{1,0:T(8,128)S(1)} %bitcast.1078, f32[5,128]{1,0:T(8,128)S(1)} %bitcast.1083, f32[5,128]{1,0:T(8,128)S(1)} %bitcast.1088, ...), kind=kLoop, calls=%fused_computation.602.clone.1 | loop fusion | flops 21461760 | bytes 163860 | tf_op jit(solution)/shard_map/while/body/reduce_sum | solution.py:260
  317.0 4.2 %fusion.252 = (f32[5,128]{1,0:T(8,128)S(1)}, f32[5,128]{1,0:T(8,128)S(1)}) fusion(f32[5,128]{1,0:T(8,128)S(1)} %bitcast.1064, f32[5,128]{1,0:T(8,128)S(1)} %bitcast.1069, f32[5,128]{1,0:T(8,128)S(1)} %bitcast.1074, f32[5,128]{1,0:T(8,128)S(1)} %bitcast.1079, f32[5,128]{1,0:T(8,128)S(1)} %bitcast.1084, f32[5,128]{1,0:T(8,128)S(1)} %bitcast.1089, ...), kind=kLoop, calls=%fused_computation.603.clone.1 | loop fusion | flops 19249920 | bytes 163860 | tf_op jit(solution)/shard_map/while/body/reduce_sum | solution.py:260
  321.2 4.5 %fusion.254 = (f32[5,128]{1,0:T(8,128)S(1)}, f32[5,128]{1,0:T(8,128)S(1)}) fusion(f32[5,128]{1,0:T(8,128)S(1)} %bitcast.1065, f32[5,128]{1,0:T(8,128)S(1)} %bitcast.1070, f32[5,128]{1,0:T(8,128)S(1)} %bitcast.1075, f32[5,128]{1,0:T(8,128)S(1)} %bitcast.1080, f32[5,128]{1,0:T(8,128)S(1)} %bitcast.1085, f32[5,128]{1,0:T(8,128)S(1)} %bitcast.1090, ...), kind=kLoop, calls=%fused_computation.601.clone.1 | loop fusion | flops 21461760 | bytes 163860 | tf_op jit(solution)/shard_map/while/body/reduce_sum | solution.py:260
  325.8 4.6 %fusion.255 = (f32[5,128]{1,0:T(8,128)S(1)}, f32[5,128]{1,0:T(8,128)S(1)}) fusion(f32[5,128]{1,0:T(8,128)S(1)} %bitcast.1066, f32[5,128]{1,0:T(8,128)S(1)} %bitcast.1071, f32[5,128]{1,0:T(8,128)S(1)} %bitcast.1076, f32[5,128]{1,0:T(8,128)S(1)} %bitcast.1081, f32[5,128]{1,0:T(8,128)S(1)} %bitcast.1086, f32[5,128]{1,0:T(8,128)S(1)} %bitcast.1091, ...), kind=kLoop, calls=%fused_computation.600.clone.1 | loop fusion | flops 21461760 | bytes 163860 | tf_op jit(solution)/shard_map/while/body/reduce_sum | solution.py:260
  330.4 5.8 %fusion.256 = (f32[5,128]{1,0:T(8,128)S(1)}, f32[5,128]{1,0:T(8,128)S(1)}) fusion(f32[5,128]{1,0:T(8,128)S(1)} %bitcast.1067, f32[5,128]{1,0:T(8,128)S(1)} %bitcast.1072, f32[5,128]{1,0:T(8,128)S(1)} %bitcast.1077, f32[5,128]{1,0:T(8,128)S(1)} %bitcast.1082, f32[5,128]{1,0:T(8,128)S(1)} %bitcast.1087, f32[5,128]{1,0:T(8,128)S(1)} %bitcast.1092, ...), kind=kLoop, calls=%fused_computation.599.clone.1 | loop fusion | flops 29735680 | bytes 163860 | tf_op jit(solution)/shard_map/while/body/reduce_sum | solution.py:260
  341.7 4.5 %fusion.253 = (f32[5,128]{1,0:T(8,128)S(1)}, f32[5,128]{1,0:T(8,128)S(1)}) fusion(f32[5,128]{1,0:T(8,128)S(1)} %bitcast.1063, f32[5,128]{1,0:T(8,128)S(1)} %bitcast.1068, f32[5,128]{1,0:T(8,128)S(1)} %bitcast.1073, f32[5,128]{1,0:T(8,128)S(1)} %bitcast.1078, f32[5,128]{1,0:T(8,128)S(1)} %bitcast.1083, f32[5,128]{1,0:T(8,128)S(1)} %bitcast.1088, ...), kind=kLoop, calls=%fused_computation.602.clone.1 | loop fusion | flops 21461760 | bytes 163860 | tf_op jit(solution)/shard_map/while/body/reduce_sum | solution.py:260
  346.1 4.2 %fusion.252 = (f32[5,128]{1,0:T(8,128)S(1)}, f32[5,128]{1,0:T(8,128)S(1)}) fusion(f32[5,128]{1,0:T(8,128)S(1)} %bitcast.1064, f32[5,128]{1,0:T(8,128)S(1)} %bitcast.1069, f32[5,128]{1,0:T(8,128)S(1)} %bitcast.1074, f32[5,128]{1,0:T(8,128)S(1)} %bitcast.1079, f32[5,128]{1,0:T(8,128)S(1)} %bitcast.1084, f32[5,128]{1,0:T(8,128)S(1)} %bitcast.1089, ...), kind=kLoop, calls=%fused_computation.603.clone.1 | loop fusion | flops 19249920 | bytes 163860 | tf_op jit(solution)/shard_map/while/body/reduce_sum | solution.py:260
  350.3 4.5 %fusion.254 = (f32[5,128]{1,0:T(8,128)S(1)}, f32[5,128]{1,0:T(8,128)S(1)}) fusion(f32[5,128]{1,0:T(8,128)S(1)} %bitcast.1065, f32[5,128]{1,0:T(8,128)S(1)} %bitcast.1070, f32[5,128]{1,0:T(8,128)S(1)} %bitcast.1075, f32[5,128]{1,0:T(8,128)S(1)} %bitcast.1080, f32[5,128]{1,0:T(8,128)S(1)} %bitcast.1085, f32[5,128]{1,0:T(8,128)S(1)} %bitcast.1090, ...), kind=kLoop, calls=%fused_computation.601.clone.1 | loop fusion | flops 21461760 | bytes 163860 | tf_op jit(solution)/shard_map/while/body/reduce_sum | solution.py:260
  354.9 4.6 %fusion.255 = (f32[5,128]{1,0:T(8,128)S(1)}, f32[5,128]{1,0:T(8,128)S(1)}) fusion(f32[5,128]{1,0:T(8,128)S(1)} %bitcast.1066, f32[5,128]{1,0:T(8,128)S(1)} %bitcast.1071, f32[5,128]{1,0:T(8,128)S(1)} %bitcast.1076, f32[5,128]{1,0:T(8,128)S(1)} %bitcast.1081, f32[5,128]{1,0:T(8,128)S(1)} %bitcast.1086, f32[5,128]{1,0:T(8,128)S(1)} %bitcast.1091, ...), kind=kLoop, calls=%fused_computation.600.clone.1 | loop fusion | flops 21461760 | bytes 163860 | tf_op jit(solution)/shard_map/while/body/reduce_sum | solution.py:260
  359.5 5.8 %fusion.256 = (f32[5,128]{1,0:T(8,128)S(1)}, f32[5,128]{1,0:T(8,128)S(1)}) fusion(f32[5,128]{1,0:T(8,128)S(1)} %bitcast.1067, f32[5,128]{1,0:T(8,128)S(1)} %bitcast.1072, f32[5,128]{1,0:T(8,128)S(1)} %bitcast.1077, f32[5,128]{1,0:T(8,128)S(1)} %bitcast.1082, f32[5,128]{1,0:T(8,128)S(1)} %bitcast.1087, f32[5,128]{1,0:T(8,128)S(1)} %bitcast.1092, ...), kind=kLoop, calls=%fused_computation.599.clone.1 | loop fusion | flops 29735680 | bytes 163860 | tf_op jit(solution)/shard_map/while/body/reduce_sum | solution.py:260
  366.4 4.8 %collective-permute-done.4 = f32[5,32,128]{2,1,0:T(8,128)S(1)} collective-permute-done((f32[5,32,128]{2,1,0:T(8,128)S(1)}, f32[5,32,128]{2,1,0:T(8,128)S(1)}, u32[]{:S(2)}, u32[]{:S(2)}) %collective-permute-start.4) | collective-permute-done | bytes 81952 | tf_op jit(solution)/shard_map/ppermute | solution.py:24
  371.8 32.8 %all-reduce.5.cloned.1.call-done = f32[5,32,128]{2,1,0:T(8,128)} async-done(((f32[5,32,128]{2,1,0:T(8,128)}), f32[5,32,128]{2,1,0:T(8,128)}) %all-reduce.5.cloned.1.call-update) | async-done | bytes 81936 | tf_op jit(solution)/shard_map/psum | solution.py:328
  404.6 0.9 multiply_bitcast_fusion.4
  (1536 shorter events, 81.2 us)
Async XLA Ops:
  6.5 117.9 %all-reduce.3.cloned.1.call-start = ((), (), s32[]{:S(2)}) async-start(), calls=%async_computation | async-start | bytes 720896 | tf_op jit(solution)/shard_map/psum | solution.py:328
  7.2 9.5 %collective-permute-start.1 = (f32[32]{0:T(128)S(1)}, f32[32]{0:T(128)S(1)}, u32[]{:S(2)}, u32[]{:S(2)}) collective-permute-start(f32[32]{0:T(128)S(1)} %convert_element_type.36), channel_id=1, source_target_pairs={{0,28},{4,0},{8,4},{12,8},{16,12},{20,16},{24,20},{28,24},{1,29},{... | collective-permute-start | bytes 392 | tf_op jit(solution)/shard_map/ppermute | solution.py:24
  10.5 1.7 copy-start.5
  11.5 5.3 %collective-permute-start = (f32[8,4096]{1,0:T(8,128)S(1)}, f32[8,4096]{1,0:T(8,128)S(1)}, u32[]{:S(2)}, u32[]{:S(2)}) collective-permute-start(f32[8,4096]{1,0:T(8,128)S(1)} %pad_maximum_fusion.2), channel_id=1, source_target_pairs={{0,28},{4,0},{8,4},{12,8},{16,12},{20,16},{24,20},{28,24},{1,29},{... | collective-permute-start | bytes 393224 | tf_op jit(solution)/shard_map/ppermute | solution.py:24
  12.2 4.6 %copy-start.4 = (f32[4096]{0:T(1024)S(1)}, f32[4096]{0:T(1024)}, u32[]{:S(2)}) copy-start(f32[4096]{0:T(1024)} %param.16) | copy-start | bytes 49156
  12.3 4.5 %copy-start.3 = (f32[4096]{0:T(1024)S(1)}, f32[4096]{0:T(1024)}, u32[]{:S(2)}) copy-start(f32[4096]{0:T(1024)} %param.17) | copy-start | bytes 49156
  14.4 2.4 copy-start.6
  14.4 2.4 copy-start.1
  14.4 2.4 copy-start.2
  81.6 7.8 %collective-permute-start.2 = (f32[22,32,128]{2,1,0:T(8,128)S(1)}, f32[22,32,128]{2,1,0:T(8,128)S(1)}, u32[]{:S(2)}, u32[]{:S(2)}) collective-permute-start(f32[22,32,128]{2,1,0:T(8,128)S(1)} %slice.766), channel_id=1, source_target_pairs={{0,4},{4,8},{8,12},{12,16},{16,20},{20,24},{24,28},{28,0},{1,5},{5... | collective-permute-start | bytes 1081352 | tf_op jit(solution)/shard_map/ppermute | solution.py:24
  90.2 314.4 %all-reduce.5.cloned.1.call-start = ((), (), s32[]{:S(2)}) async-start(), calls=%async_computation.1 | async-start | bytes 163840 | tf_op jit(solution)/shard_map/psum | solution.py:328
  125.3 1.1 copy-start
  126.7 5.3 %collective-permute-start.3 = (f32[22,32,128]{2,1,0:T(8,128)S(1)}, f32[22,32,128]{2,1,0:T(8,128)S(1)}, u32[]{:S(2)}, u32[]{:S(2)}) collective-permute-start(f32[22,32,128]{2,1,0:T(8,128)S(1)} %constant_dynamic-update-slice_fusion.54), channel_id=1, source_target_pairs={{0,28},{4,0},{8,4},{12,8},{16,12},{20,16},{24,20},{28,24},{1,29},{... | collective-permute-start | bytes 1081352 | tf_op jit(solution)/shard_map/ppermute | solution.py:24
  366.3 4.8 %collective-permute-start.4 = (f32[5,32,128]{2,1,0:T(8,128)S(1)}, f32[5,32,128]{2,1,0:T(8,128)S(1)}, u32[]{:S(2)}, u32[]{:S(2)}) collective-permute-start(f32[5,32,128]{2,1,0:T(8,128)S(1)} %slice.791), channel_id=1, source_target_pairs={{0,4},{4,8},{8,12},{12,16},{16,20},{20,24},{24,28},{28,0},{1,5},{5... | collective-permute-start | bytes 245768 | tf_op jit(solution)/shard_map/ppermute | solution.py:24
Sparse Core Ops, SparseCore 0:
  90.3 34.1 all-reduce.2
  371.9 32.6 all-reduce.4
where the time goes:
time: 414 us; the launch traced here: 413 us
  other arithmetic  234 us (57%)
  waiting for transfers between devices  84.5 us (20%)
  local copies, waits for them, and re-layouts  62.7 us (15%)
  between operations  14.4 us (3%)
  loops' own time  10.6 us (3%)
  starting transfers between devices  4.6 us (1%)
    reduce_sum x40, other arithmetic, flux_tile(): jnp.sum(pair_scale * face_flux, axis=1)  188 us
    psum x2, waiting for transfers between devices, settle(): merged = lax.psum(merged, 'sub')  67.1 us
    reduce_sum x16, other arithmetic, moment_tile(): col_sums = jnp.stack([jnp.sum(summand, axis=1) for summand in summands])  29.6 us
    ppermute x5, waiting for transfers between devices, shifted(): lax.ppermute(shard, axis, [(i, (i + by) % peers) for i in range(peers)])  17.4 us
    another operation x2, loops' own time, sweep(): row_buffer, col_buffer = lax.fori_loop(0, turns, one_turn, (empty, empty))  10.6 us
  transfers between devices with their start and end apart: 7, of which 5 were waited for; matrix products, arithmetic and copies ran while one was open for 1% of the time, Pallas kernels for 0%

commit v1 on v0

v1 whole, which is shorter than its diff:
```python
import functools
import math

import jax
import jax.numpy as jnp
from jax import lax
from jax.experimental import pallas as pl
from jax.experimental.pallas import tpu as pltpu
from jax.sharding import PartitionSpec as P

LEAF = 128
CAND = 5

GAMMA = 5.0 / 3.0
SUPPORT = 1.5
KERNEL_NORM = 21.0 / (2.0 * math.pi * SUPPORT**3)
MOMENT_REG = 0.05
AREA_FLOOR = 0.0001
AWAY = 64.0
UNROLL = 4
F32 = jnp.float32
BF16 = jnp.bfloat16


def shifted(shard, axis, by):
    peers = lax.axis_size(axis)
    return lax.ppermute(shard, axis, [(i, (i + by) % peers) for i in range(peers)])


def swapped(shard, axis, mask):
    peers = lax.axis_size(axis)
    return lax.ppermute(shard, axis, [(i, i ^ mask) for i in range(peers)])


def reciprocal(value):
    guess = pl.reciprocal(value, approx=True)
    return guess * (2.0 - value * guess)


def smoothing_of(dist_sq, scale):
    safe = jnp.maximum(dist_sq, 1e-12)
    radius = safe * lax.rsqrt(safe)
    inside = jnp.maximum(1.0 - radius * (1.0 / SUPPORT), 0.0)
    square = inside * inside
    return (square * square) * (scale + (scale * (4.0 / SUPPORT)) * radius)


def split_three(value):
    high = value.astype(BF16).astype(F32)
    rest = value - high
    middle = rest.astype(BF16).astype(F32)
    return high, middle, rest - middle


def bilinear(near_rows, far_rows):
    near_high, near_mid, near_low = split_three(near_rows)
    far_high, far_mid, far_low = split_three(far_rows)
    near_stack = jnp.concatenate(
        [near_high, near_high, near_high, near_mid, near_mid, near_low], axis=0
    ).astype(BF16)
    far_stack = jnp.concatenate(
        [far_high, far_mid, far_low, far_high, far_mid, far_high], axis=0
    ).astype(BF16)
    return lax.dot_general(
        near_stack, far_stack, (((0,), (0,)), ((), ())), preferred_element_type=F32
    )


def moment_features(tile):
    row = lax.broadcasted_iota(jnp.int32, tile.shape, 0)
    by_x = tile * tile[0:1]
    by_y = jnp.where(row == 0, 1.0, tile * tile[1:2])
    by_z = tile * tile[2:3]
    whole = jnp.concatenate([tile, by_x, by_y, by_z], axis=0)
    high = whole.astype(BF16)
    low = (whole - high.astype(F32)).astype(BF16)
    both = jnp.concatenate([high, low], axis=0)
    return jnp.concatenate([both, both], axis=1)


def displacement(step_x, step_y, wrap):
    row = lax.broadcasted_iota(jnp.int32, (8, LEAF), 0)
    zero = jnp.zeros((8, LEAF), F32)
    out = jnp.where(row == 0, step_x, zero)
    out = jnp.where(row == 1, step_y, out)
    return jnp.where(row == 4, -wrap, out)


def finish_leaf(raw, tile):
    pos = [tile[k : k + 1] for k in range(3)]
    live = pos[0] < 0.5 * AWAY
    total = raw[16:17]
    first = [raw[k : k + 1] - pos[k] * total for k in range(3)]

    def second(left, right):
        lead = raw[8 + 8 * left + right : 9 + 8 * left + right]
        return lead - pos[left] * raw[right : right + 1] - pos[right] * first[left]

    density = jnp.where(live, total, 1.0)
    inverse_density = 1.0 / density

    def scaled(value):
        return jnp.where(live, value * inverse_density, 0.0)

    exx = scaled(second(0, 0)) + MOMENT_REG
    exy = scaled(second(0, 1))
    exz = scaled(second(0, 2))
    eyy = scaled(second(1, 1)) + MOMENT_REG
    eyz = scaled(second(1, 2))
    ezz = scaled(second(2, 2)) + MOMENT_REG
    mxx = eyy * ezz - eyz * eyz
    mxy = exz * eyz - exy * ezz
    mxz = exy * eyz - exz * eyy
    myy = exx * ezz - exz * exz
    myz = exy * exz - exx * eyz
    mzz = exx * eyy - exy * exy
    scale = 1.0 / (exx * mxx + exy * mxy + exz * mxz)
    inverse = [entry * scale for entry in (mxx, mxy, mxz, myy, myz, mzz)]
    square = inverse_density * inverse_density
    rows = [density] + [entry * square for entry in inverse]
    for quantity in range(3, 8):
        value = tile[quantity : quantity + 1]
        along = [
            scaled(
                raw[8 + 8 * k + quantity : 9 + 8 * k + quantity]
                - pos[k] * raw[quantity : quantity + 1]
                - value * first[k]
            )
            for k in range(3)
        ]
        half = [0.5 * term for term in along]
        rows.append(inverse[0] * half[0] + inverse[1] * half[1] + inverse[2] * half[2])
        rows.append(inverse[1] * half[0] + inverse[3] * half[1] + inverse[4] * half[2])
        rows.append(inverse[2] * half[0] + inverse[4] * half[1] + inverse[5] * half[2])
    rows.append(jnp.zeros((2, LEAF), F32))
    return jnp.concatenate(rows, axis=0)


def dot3(left, right):
    return left[0] * right[0] + left[1] * right[1] + left[2] * right[2]


def apply_sym(matrix, vector):
    return [
        dot3((matrix[0], matrix[1], matrix[2]), vector),
        dot3((matrix[1], matrix[3], matrix[4]), vector),
        dot3((matrix[2], matrix[4], matrix[5]), vector),
    ]


def limited(value, low, high):
    return jnp.minimum(jnp.maximum(value, low), high)


def face_fluxes(near, far, weight):
    sep = [far[k] - near[k] for k in range(3)]
    smooth = smoothing_of(dot3(sep, sep), KERNEL_NORM)
    toward = apply_sym([near[8 + k] + far[8 + k] for k in range(6)], sep)
    length_sq = jnp.maximum(dot3(toward, toward), 1e-30)
    inverse_length = lax.rsqrt(length_sq)
    magnitude = smooth * (length_sq * inverse_length)
    scale = jnp.minimum(inverse_length, smooth * (1.0 / AREA_FLOOR))
    normal = [entry * scale for entry in toward]
    left_vel, right_vel, face_vel = [], [], []
    for k in range(3):
        face_vel.append(0.5 * (near[3 + k] + far[3 + k]))
        half_gap = 0.5 * (far[3 + k] - near[3 + k])
        high = jnp.abs(half_gap)
        low = -high
        left_vel.append(limited(dot3(near[14 + 3 * k : 17 + 3 * k], sep) - half_gap, low, high))
        right_vel.append(limited(half_gap - dot3(far[14 + 3 * k : 17 + 3 * k], sep), low, high))
    thermo = []
    for k in (3, 4):
        low = jnp.minimum(near[3 + k], far[3 + k])
        high = jnp.maximum(near[3 + k], far[3 + k])
        thermo.append(
            limited(near[3 + k] + dot3(near[14 + 3 * k : 17 + 3 * k], sep), low, high)
        )
        thermo.append(
            limited(far[3 + k] - dot3(far[14 + 3 * k : 17 + 3 * k], sep), low, high)
        )
    left_rho, right_rho, left_p, right_p = thermo
    left_u = dot3(left_vel, normal)
    right_u = dot3(right_vel, normal)
    left_gp = GAMMA * left_p
    right_gp = GAMMA * right_p
    left_c = left_gp * lax.rsqrt(left_gp * left_rho)
    right_c = right_gp * lax.rsqrt(right_gp * right_rho)
    slow = jnp.minimum(left_u - left_c, right_u - right_c)
    fast = jnp.maximum(left_u + left_c, right_u + right_c)
    left_m = left_rho * (slow - left_u)
    right_m = right_rho * (fast - right_u)
    contact = (right_p - left_p + left_m * left_u - right_m * right_u) * reciprocal(
        left_m - right_m
    )
    is_left = contact >= 0.0
    speed = jnp.where(is_left, jnp.minimum(slow, 0.0), jnp.maximum(fast, 0.0))
    rho = jnp.where(is_left, left_rho, right_rho)
    press = jnp.where(is_left, left_p, right_p)
    normal_speed = jnp.where(is_left, left_u, right_u)
    vel = [jnp.where(is_left, left_vel[k], right_vel[k]) for k in range(3)]
    lag = speed - normal_speed
    ratio = lag * reciprocal(speed - contact)
    through = ratio * contact
    gain = speed * ratio - speed
    push = (rho * lag) * gain
    area = magnitude * weight
    mass = (rho * through) * area
    total_p = (press + push) * area
    mom = [mass * vel[k] + total_p * normal[k] for k in range(3)]
    energy = (press * (through * (1.0 / (GAMMA - 1.0)) + normal_speed + gain) + push * contact) * area
    energy = energy + (0.5 * dot3(vel, vel)) * mass
    energy = energy + dot3(face_vel, mom) + (0.5 * dot3(face_vel, face_vel)) * mass
    return [mass] + [mom[k] + face_vel[k] * mass for k in range(3)] + [energy]


def step_kernel(
    width,
    leaf_sub,
    slot_count,
    own_first,
    own_slots,
    rec,
    info,
    lower_ref,
    own_ref,
    upper_ref,
    beyond_ref,
    own_out,
    next_out,
    order,
    local,
    raw,
    pay,
    near_cols,
    far_rows,
    col_sum,
    row_sum,
):
    whole = 4 * width

    def load_leaf(column, carry):
        lanes = pl.ds(pl.multiple_of(column * LEAF, LEAF), LEAF)
        local[column] = lower_ref[:, lanes]
        local[width + column] = own_ref[:, lanes]
        local[2 * width + column] = upper_ref[:, lanes]
        local[3 * width + column] = beyond_ref[:, lanes]
        own_out[:, lanes] = jnp.zeros((5, LEAF), F32)
        next_out[:, lanes] = jnp.zeros((5, LEAF), F32)
        col_sum[column] = jnp.zeros((8, LEAF), F32)
        col_sum[width + column] = jnp.zeros((8, LEAF), F32)
        for slab in range(4):
            raw[slab * width + column] = jnp.zeros((32, LEAF), F32)
        return carry

    lax.fori_loop(0, width, load_leaf, 0)
    local[whole] = jnp.zeros((8, LEAF), F32)
    raw[whole] = jnp.zeros((32, LEAF), F32)
    for home in range(leaf_sub):
        row_sum[home] = jnp.zeros((LEAF, LEAF), F32)

    def collect(slot, used):
        order[used] = slot
        return used + rec[5, slot]

    used = lax.fori_loop(0, slot_count, collect, 0, unroll=8)
    for extra in range(UNROLL):
        order[used + extra] = slot_count

    def moment_slot(slot):
        home = rec[0, slot]
        other = rec[1, slot]
        shift = displacement(
            rec[2, slot].astype(F32), rec[3, slot].astype(F32), rec[4, slot].astype(F32)
        )
        near = local[home]
        far = local[other] + shift
        weight = jnp.where(home == other, 0.5, 1.0).astype(F32)
        row = lax.broadcasted_iota(jnp.int32, (8, LEAF), 0)
        near_sq = dot3([near[k : k + 1] for k in range(3)], [near[k : k + 1] for k in range(3)])
        far_sq = dot3([far[k : k + 1] for k in range(3)], [far[k : k + 1] for k in range(3)])
        near_k = jnp.where(row < 3, near, jnp.where(row == 3, near_sq, jnp.where(row == 4, 1.0, 0.0)))
        far_k = jnp.where(
            row < 3, -2.0 * far, jnp.where(row == 4, far_sq, jnp.where(row == 3, 1.0, 0.0))
        )
        smooth = smoothing_of(bilinear(near_k, far_k), KERNEL_NORM * weight)
        high = smooth.astype(BF16)
        low = (smooth - high.astype(F32)).astype(BF16)
        row_part = lax.dot_general(
            moment_features(far),
            jnp.concatenate([high, low], axis=1),
            (((1,), (1,)), ((), ())),
            preferred_element_type=F32,
        )
        col_part = lax.dot_general(
            moment_features(near - shift),
            jnp.concatenate([high, low], axis=0),
            (((1,), (0,)), ((), ())),
            preferred_element_type=F32,
        )
        return home, other, row_part[:32] + row_part[32:], col_part[:32] + col_part[32:]

    def moment_group(group, carry):
        parts = [moment_slot(order[group * UNROLL + k]) for k in range(UNROLL)]
        for home, other, row_part, col_part in parts:
            raw[home] += row_part
            raw[other] += col_part
        return carry

    lax.fori_loop(0, (used + UNROLL - 1) // UNROLL, moment_group, 0)

    base = info[0]
    upper_base = info[1]

    def own_leaf(k):
        return width + lax.rem(base + k, width)

    def upper_leaf(k):
        return 2 * width + lax.rem(upper_base + k, width)

    def finish(leaf):
        pay[leaf] = finish_leaf(raw[leaf], local[leaf])

    def finish_own(k, carry):
        finish(own_leaf(k))
        return carry

    def finish_upper(k, carry):
        finish(upper_leaf(k))
        return carry

    lax.fori_loop(0, leaf_sub + 1, finish_own, 0)
    lax.fori_loop(0, leaf_sub + 2, finish_upper, 0)

    def turn_home(k, carry):
        leaf = own_leaf(k)
        rows = jnp.concatenate(
            [local[leaf], pay[leaf], jnp.zeros((LEAF - 32, LEAF), F32)], axis=0
        )
        near_cols[k] = rows.T
        return carry

    lax.fori_loop(0, leaf_sub, turn_home, 0)

    lane = lax.broadcasted_iota(jnp.int32, (8, LEAF), 1)

    def flux_slot(slot, carry):
        home = rec[0, slot]
        other = rec[1, slot]
        live = rec[6, slot]

        @pl.when(live > 0)
        def _():
            shift = displacement(
                rec[2, slot].astype(F32), rec[3, slot].astype(F32), rec[4, slot].astype(F32)
            )
            far_rows[0:8] = local[other] + shift
            far_rows[8:32] = pay[other]
            weight = jnp.where(home == other, 0.5, 1.0).astype(F32)
            home_column = home - width
            seat = home_column - base
            blocks = (info[8 + home_column] + 7) // 8
            picks = list(range(8)) + list(range(9, 30))

            def row_block(block, sums):
                rows = pl.ds(pl.multiple_of(block * 8, 8), 8)
                cols = near_cols[seat, rows, :]
                near = [jnp.broadcast_to(cols[:, k : k + 1], (8, LEAF)) for k in picks]
                far = [jnp.broadcast_to(far_rows[k : k + 1, :], (8, LEAF)) for k in picks]
                fluxes = face_fluxes(near, far, weight)
                gathered = row_sum[seat, rows, :]
                for k in range(5):
                    part = jnp.sum(fluxes[k], axis=1, keepdims=True)
                    gathered = gathered + jnp.where(lane == k, part, 0.0)
                row_sum[seat, rows, :] = gathered
                return tuple(sums[k] + fluxes[k] for k in range(5))

            sums = lax.fori_loop(
                0, blocks, row_block, tuple(jnp.zeros((8, LEAF), F32) for _ in range(5))
            )
            flat = [jnp.sum(entry, axis=0, keepdims=True) for entry in sums]
            col_sum[other - width] += jnp.concatenate(flat + [jnp.zeros((3, LEAF), F32)], axis=0)

        return carry

    lax.fori_loop(own_first, own_first + own_slots, flux_slot, 0)

    def subtract_rows(k, carry):
        column = own_leaf(k) - width
        col_sum[column] = col_sum[column] - row_sum[k].T[0:8]
        return carry

    lax.fori_loop(0, leaf_sub, subtract_rows, 0)

    def rates(leaf):
        live = local[leaf][0:1] < 0.5 * AWAY
        total = col_sum[leaf - width] * pay[leaf][0:1]
        return jnp.where(live, total, 0.0)[0:5]

    def write_own(k, carry):
        leaf = own_leaf(k)
        own_out[:, pl.ds(pl.multiple_of((leaf - width) * LEAF, LEAF), LEAF)] = rates(leaf)
        return carry

    def write_upper(k, carry):
        leaf = upper_leaf(k)
        next_out[:, pl.ds(pl.multiple_of((leaf - 2 * width) * LEAF, LEAF), LEAF)] = rates(leaf)
        return carry

    lax.fori_loop(0, leaf_sub + 1, write_own, 0)
    lax.fori_loop(0, leaf_sub + 2, write_upper, 0)


def shards(positions, velocity, density, pressure, counts, pair_list):
    width = counts.shape[0]
    slots = pair_list.shape[1]
    particles = width * LEAF
    sub_count = lax.axis_size("sub")
    leaf_sub = width // sub_count
    slab_index = lax.axis_index("slab")
    sub_index = lax.axis_index("sub")

    particle = jnp.arange(particles, dtype=jnp.int32)
    column = particle // LEAF
    live = (particle % LEAF) < jnp.repeat(counts, LEAF, total_repeat_length=particles)
    centre_x = slab_index.astype(F32) + 0.5
    local_x = jnp.where(live, positions[0] - centre_x, AWAY)
    local_y = positions[1] - (column.astype(F32) + 0.5)
    local_z = positions[2] - 0.5
    state = jnp.concatenate(
        [local_x[None], local_y[None], local_z[None], velocity, density[None], pressure[None]], axis=0
    )
    misc = pair_list.reshape(-1).astype(F32)
    lanes = -(-misc.shape[0] // (8 * LEAF)) * LEAF
    misc = jnp.pad(misc, (0, 8 * lanes - misc.shape[0])).reshape(8, lanes)
    packed = jnp.concatenate([state, misc], axis=1)
    lower = shifted(packed, "slab", 1)
    upper = shifted(packed, "slab", -1)
    beyond = shifted(packed, "slab", -2)

    lists = jnp.stack([lower[:, particles:], packed[:, particles:], upper[:, particles:]])
    lists = lists.reshape(3, -1)[:, : 3 * slots].reshape(1, 3, 3, slots)
    mask = 1
    while mask < sub_count:
        lists = jnp.concatenate([lists, swapped(lists, "sub", mask)], axis=0)
        mask *= 2
    lists = lists.astype(jnp.int32)
    head, tail, offset = lists[:, :, 0], lists[:, :, 1], lists[:, :, 2]
    occupied = head >= 0
    head = jnp.where(occupied, head, 0)
    tail = jnp.where(occupied, tail, 0)
    head_col, tail_col = head % width, tail % width
    step_x = (head // width != tail // width).astype(jnp.int32)
    wrap = (tail // width < head // width).astype(jnp.int32)
    from_slab = jnp.arange(3, dtype=jnp.int32)[None, :, None]
    home = from_slab * width + head_col
    other = (from_slab + step_x) * width + tail_col
    step_y = tail_col + offset - head_col
    own_shift = jnp.max(
        jnp.where(occupied[0, 1] & (step_x[0, 1] > 0), (-offset[0, 1]) % width, 0)
    )
    base = sub_index * leaf_sub
    upper_base = (base - 1 + own_shift) % width

    def wanted(leaf_slab, leaf_column):
        in_own = (leaf_slab == 1) & ((leaf_column - base) % width <= leaf_sub)
        in_upper = (leaf_slab == 2) & ((leaf_column - upper_base) % width <= leaf_sub + 1)
        return in_own | in_upper

    needed = occupied & (wanted(from_slab, head_col) | wanted(from_slab + step_x, tail_col))
    slot_count = sub_count * 3 * slots
    rec = jnp.stack(
        [
            jnp.broadcast_to(entry, head.shape).reshape(-1)
            for entry in (
                home,
                other,
                step_x,
                step_y,
                wrap,
                needed.astype(jnp.int32),
                occupied.astype(jnp.int32),
            )
        ]
    )
    spare = jnp.array([[4 * width], [4 * width], [0], [0], [0], [0], [0]], jnp.int32)
    rec = jnp.concatenate([rec, spare], axis=1)
    info = jnp.concatenate(
        [base[None], upper_base[None], jnp.zeros((6,), jnp.int32), counts]
    ).astype(jnp.int32)

    smem = pl.BlockSpec(memory_space=pltpu.SMEM)
    vmem = pl.BlockSpec(memory_space=pltpu.VMEM)
    own_part, next_part = pl.pallas_call(
        functools.partial(step_kernel, width, leaf_sub, slot_count, slots, slots),
        out_shape=[jax.ShapeDtypeStruct((5, particles), F32)] * 2,
        in_specs=[smem, smem, vmem, vmem, vmem, vmem],
        out_specs=[vmem, vmem],
        scratch_shapes=[
            pltpu.SMEM((slot_count + UNROLL + 1,), jnp.int32),
            pltpu.VMEM((4 * width + 1, 8, LEAF), F32),
            pltpu.VMEM((4 * width + 1, 32, LEAF), F32),
            pltpu.VMEM((4 * width, 24, LEAF), F32),
            pltpu.VMEM((leaf_sub, LEAF, LEAF), F32),
            pltpu.VMEM((32, LEAF), F32),
            pltpu.VMEM((2 * width, 8, LEAF), F32),
            pltpu.VMEM((leaf_sub, LEAF, LEAF), F32),
        ],
        compiler_params=pltpu.CompilerParams(vmem_limit_bytes=48 * 1024 * 1024),
        name="hydro_step",
    )(rec, info, lower, packed, upper, beyond)

    merged = own_part + shifted(next_part, "slab", 1)
    mask = 1
    while mask < sub_count:
        merged = merged + swapped(merged, "sub", mask)
        mask *= 2
    return merged


def solution(mesh):
    placed = (
        P(None, "slab"),
        P(None, "slab"),
        P("slab"),
        P("slab"),
        P("slab"),
        P(None, ("slab", "sub")),
    )
    return jax.shard_map(
        shards, mesh=mesh, in_specs=placed, out_specs=P(None, "slab"), check_vma=False
    )
```

time: 414 us -> 234 us (0.57)
  the two profiles are of different devices: /device:TPU:0 before, /device:TPU:2 now
where the time goes in v1:
time: 234 us; the launch traced here: 229 us
  starting transfers between devices  112 us (48%)
  Pallas kernels  68.8 us (29%)
  other arithmetic  23.4 us (10%)
  waiting for transfers between devices  18.9 us (8%)
  local copies, waits for them, and re-layouts  5.35 us (2%)
    ppermute x4, starting transfers between devices, swapped(): return lax.ppermute(shard, axis, [(i, i ^ mask) for i in range(peers)])  109 us
    pallas_call x1, Pallas kernels, shards(): pl.pallas_call(functools.partial(step_kernel, width, leaf_sub, slot_count...  68.8 us
    gather x3, other arithmetic, shards(): jnp.repeat(counts, LEAF, total_repeat_length=particles)  21.4 us
    ppermute x4, waiting for transfers between devices, swapped(): return lax.ppermute(shard, axis, [(i, i ^ mask) for i in range(peers)])  11.9 us
    ppermute x4, waiting for transfers between devices, shifted(): lax.ppermute(shard, axis, [(i, (i + by) % peers) for i in range(peers)])  7.01 us
  transfers between devices with their start and end apart: 8, of which 7 were waited for; matrix products, arithmetic and copies ran while one was open for 1% of the time, Pallas kernels for 0%

profile of v1, /device:TPU:2, one launch (start us, length us, event | category | flops | bytes accessed | tf_op | source)
XLA Modules:
  0.0 229.4 jit_solution(16976271388411983992)
XLA Ops:
  0.0 0.0 copy-start
  0.0 0.7 copy-done
  0.7 0.7 fusion.22
  1.4 0.7 fusion.21
  2.1 0.0 copy-start.6
  2.1 0.7 copy-done.6
  2.8 0.1 convert_element_type.75
  2.9 4.4 %compare_select_fusion.2 = (s32[4096,1]{0,1:T(1,128)S(1)}, s32[4096,1]{0,1:T(1,128)S(1)}) fusion(s32[]{:T(128)} %bitcast.29, s32[]{:T(128)} %bitcast.30, s32[]{:T(128)} %bitcast.31, s32[]{:T(128)} %bitcast.32, s32[]{:T(128)} %bitcast.33, s32[]{:T(128)} %bitcast.35, s32[]{:T(128)} %bitcast.34, s32[4096,1]{0,1:T(1,128)S(1)} %bitcast.72, s32[4096,1]{0,1:T(1,128)S(1)} %bitcast.70), kind=kLoop, calls=%fused_computation.28 | loop fusion | flops 57344 | bytes 65564 | tf_op jit(solution)/shard_map/jit(_take)/gather | solution.py:425
  7.3 1.2 compare_reduce_fusion.24
  8.5 0.0 copy-start.2
  8.5 15.8 %select_select_fusion = s32[4096]{0:T(1024)S(1)} fusion(pred[4096]{0:T(1024)(128)(4,1)S(1)} %get-tuple-element.45, pred[4096]{0:T(1024)(128)(4,1)S(1)} %get-tuple-element.44, pred[4096]{0:T(1024)(128)(4,1)S(1)} %get-tuple-element.43, pred[4096]{0:T(1024)(128)(4,1)S(1)} %get-tuple-element.42, pred[4096]{0:T(1024)(128)(4,1)S(1)} %get-tuple-element.41, ...), kind=kLoop, calls=%fused_computation.44 | loop fusion | flops 102400 | bytes 135268 | tf_op jit(solution)/shard_map/jit(_take)/gather | solution.py:425
  24.4 0.0 copy-done.2
  24.4 0.0 copy-start.1
  24.4 0.0 copy-start.3
  24.4 0.0 copy-start.4
  24.4 0.1 slice_add_fusion
  24.5 0.7 copy-done.1
  25.2 0.0 copy-done.3
  25.2 0.0 copy-done.4
  25.2 0.2 concatenate.24
  25.4 0.1 collective-permute-start.1
  25.5 0.5 collective-permute-start
  26.0 1.9 collective-permute-start.4
  27.9 0.1 collective-permute-done.1.upper_ref
  28.0 2.5 %collective-permute-done.lower_ref = f32[8,4224]{1,0:T(8,128)S(1)} collective-permute-done((f32[8,4224]{1,0:T(8,128)S(1)}, f32[8,4224]{1,0:T(8,128)S(1)}, u32[]{:S(2)}, u32[]{:S(2)}) %collective-permute-start) | collective-permute-done | bytes 135200 | tf_op jit(solution)/shard_map/ppermute | solution.py:27
  30.5 0.1 reshape.695
  30.6 1.6 collective-permute-start.2
  32.2 2.0 collective-permute-done.2
  34.2 2.6 %collective-permute-start.3 = (f32[2,3,3,40]{3,2,1,0:T(4,128)S(1)}, f32[2,3,3,40]{3,2,1,0:T(4,128)S(1)}, u32[]{:S(2)}, u32[]{:S(2)}) collective-permute-start(f32[2,3,3,40]{3,2,1,0:T(4,128)S(1)} %pad_maximum_fusion.1), channel_id=1, source_target_pairs={{0,2},{1,3},{2,0},{3,1},{4,6},{5,7},{6,4},{7,5},{8,10},{9,11},{10,... | collective-permute-start | bytes 8648 | tf_op jit(solution)/shard_map/ppermute | solution.py:32
  36.8 0.1 and.357
  36.9 0.1 and.358
  37.0 0.1 and.353
  37.1 0.1 and.354
  37.2 0.1 add.310
  37.3 0.1 add.311
  37.4 0.1 add.323
  37.5 1.4 collective-permute-done.3
  38.8 0.1 fusion.18
  39.0 0.7 fusion.14
  40.4 0.1 squeeze.24
  40.5 0.1 squeeze.23
  40.6 0.1 squeeze.25
  40.7 0.1 and_convert_fusion
  40.8 0.1 pad_add_fusion.1.info
  40.9 0.0 copy-start.5
  41.0 0.7 copy-done.5
  41.6 0.1 pad_add_fusion.rec
  41.7 0.0 collective-permute-done.4.beyond_ref
  41.7 68.8 %hydro_step.1 = (f32[5,4096]{1,0:T(8,128)S(1)}, f32[5,4096]{1,0:T(8,128)S(1)}) custom-call(s32[7,481]{1,0:T(8,128)S(1)} %pad_add_fusion.rec, s32[40]{0:T(128)S(1)} %pad_add_fusion.1.info, f32[8,4224]{1,0:T(8,128)S(1)} %collective-permute-done.lower_ref, f32[8,4224]{1,0:T(8,128)S(1)} %pad_maximum_fusion.own_ref, ...), custom_call_target="tpu_custom_call" | custom-call | tf_op jit(solution)/shard_map/hydro_step/pallas_call | solution.py:494
  110.5 0.1 collective-permute-start.5
  110.6 4.4 %collective-permute-done.5 = f32[5,4096]{1,0:T(8,128)S(1)} collective-permute-done((f32[5,4096]{1,0:T(8,128)S(1)}, f32[5,4096]{1,0:T(8,128)S(1)}, u32[]{:S(2)}, u32[]{:S(2)}) %collective-permute-start.5) | collective-permute-done | bytes 81952 | tf_op jit(solution)/shard_map/ppermute | solution.py:27
  115.0 89.0 %collective-permute-start.6 = (f32[5,4096]{1,0:T(8,128)S(1)}, f32[5,4096]{1,0:T(8,128)S(1)}, u32[]{:S(2)}, u32[]{:S(2)}) collective-permute-start(f32[5,4096]{1,0:T(8,128)S(1)} %add.335), channel_id=1, source_target_pairs={{0,1},{1,0},{2,3},{3,2},{4,5},{5,4},{6,7},{7,6},{8,9},{9,8},{10,11... | collective-permute-start | bytes 245768 | tf_op jit(solution)/shard_map/ppermute | solution.py:32
  204.0 4.1 %collective-permute-done.6 = f32[5,4096]{1,0:T(8,128)S(1)} collective-permute-done((f32[5,4096]{1,0:T(8,128)S(1)}, f32[5,4096]{1,0:T(8,128)S(1)}, u32[]{:S(2)}, u32[]{:S(2)}) %collective-permute-start.6) | collective-permute-done | bytes 81952 | tf_op jit(solution)/shard_map/ppermute | solution.py:32
  208.1 16.3 %collective-permute-start.7 = (f32[5,4096]{1,0:T(8,128)S(1)}, f32[5,4096]{1,0:T(8,128)S(1)}, u32[]{:S(2)}, u32[]{:S(2)}) collective-permute-start(f32[5,4096]{1,0:T(8,128)S(1)} %add.336), channel_id=1, source_target_pairs={{0,2},{1,3},{2,0},{3,1},{4,6},{5,7},{6,4},{7,5},{8,10},{9,11},{10,... | collective-permute-start | bytes 245768 | tf_op jit(solution)/shard_map/ppermute | solution.py:32
  224.4 4.4 %collective-permute-done.7 = f32[5,4096]{1,0:T(8,128)S(1)} collective-permute-done((f32[5,4096]{1,0:T(8,128)S(1)}, f32[5,4096]{1,0:T(8,128)S(1)}, u32[]{:S(2)}, u32[]{:S(2)}) %collective-permute-start.7) | collective-permute-done | bytes 81952 | tf_op jit(solution)/shard_map/ppermute | solution.py:32
  228.8 0.7 add.337
  (23 shorter events, 0.2 us)
Async XLA Ops:
  0.0 0.7 copy-start
  2.1 0.7 copy-start.6
  8.5 15.8 %copy-start.2 = (f32[3,4096]{1,0:T(4,128)S(1)}, f32[3,4096]{1,0:T(4,128)}, u32[]{:S(2)}) copy-start(f32[3,4096]{1,0:T(4,128)} %param.9) | copy-start | bytes 147460
  24.4 0.8 copy-start.1
  24.4 0.8 copy-start.3
  24.4 0.8 copy-start.4
  25.4 2.6 %collective-permute-start.1 = (f32[8,4224]{1,0:T(8,128)S(1)}, f32[8,4224]{1,0:T(8,128)S(1)}, u32[]{:S(2)}, u32[]{:S(2)}) collective-permute-start(f32[8,4224]{1,0:T(8,128)S(1)} %pad_maximum_fusion.own_ref), channel_id=1, source_target_pairs={{0,28},{4,0},{8,4},{12,8},{16,12},{20,16},{24,20},{28,24},{1,29},{... | collective-permute-start | bytes 405512 | tf_op jit(solution)/shard_map/ppermute | solution.py:27
  25.5 5.0 %collective-permute-start = (f32[8,4224]{1,0:T(8,128)S(1)}, f32[8,4224]{1,0:T(8,128)S(1)}, u32[]{:S(2)}, u32[]{:S(2)}) collective-permute-start(f32[8,4224]{1,0:T(8,128)S(1)} %pad_maximum_fusion.own_ref), channel_id=1, source_target_pairs={{0,4},{4,8},{8,12},{12,16},{16,20},{20,24},{24,28},{28,0},{1,5},{5... | collective-permute-start | bytes 405512 | tf_op jit(solution)/shard_map/ppermute | solution.py:27
  26.0 15.7 %collective-permute-start.4 = (f32[8,4224]{1,0:T(8,128)S(1)}, f32[8,4224]{1,0:T(8,128)S(1)}, u32[]{:S(2)}, u32[]{:S(2)}) collective-permute-start(f32[8,4224]{1,0:T(8,128)S(1)} %pad_maximum_fusion.own_ref), channel_id=1, source_target_pairs={{0,24},{4,28},{8,0},{12,4},{16,8},{20,12},{24,16},{28,20},{1,25},{... | collective-permute-start | bytes 405512 | tf_op jit(solution)/shard_map/ppermute | solution.py:27
  30.6 3.6 %collective-permute-start.2 = (f32[1,3,3,40]{3,2,1,0:T(4,128)S(1)}, f32[1,3,3,40]{3,2,1,0:T(4,128)S(1)}, u32[]{:S(2)}, u32[]{:S(2)}) collective-permute-start(f32[1,3,3,40]{3,2,1,0:T(4,128)S(1)} %reshape.695), channel_id=1, source_target_pairs={{0,1},{1,0},{2,3},{3,2},{4,5},{5,4},{6,7},{7,6},{8,9},{9,8},{10,11... | collective-permute-start | bytes 4328 | tf_op jit(solution)/shard_map/ppermute | solution.py:32
  34.2 4.6 %collective-permute-start.3 = (f32[2,3,3,40]{3,2,1,0:T(4,128)S(1)}, f32[2,3,3,40]{3,2,1,0:T(4,128)S(1)}, u32[]{:S(2)}, u32[]{:S(2)}) collective-permute-start(f32[2,3,3,40]{3,2,1,0:T(4,128)S(1)} %pad_maximum_fusion.1), channel_id=1, source_target_pairs={{0,2},{1,3},{2,0},{3,1},{4,6},{5,7},{6,4},{7,5},{8,10},{9,11},{10,... | collective-permute-start | bytes 8648 | tf_op jit(solution)/shard_map/ppermute | solution.py:32
  40.9 0.7 copy-start.5
  110.5 4.4 %collective-permute-start.5 = (f32[5,4096]{1,0:T(8,128)S(1)}, f32[5,4096]{1,0:T(8,128)S(1)}, u32[]{:S(2)}, u32[]{:S(2)}) collective-permute-start(f32[5,4096]{1,0:T(8,128)S(1)} %get-tuple-element.20), channel_id=1, source_target_pairs={{0,4},{4,8},{8,12},{12,16},{16,20},{20,24},{24,28},{28,0},{1,5},{5... | collective-permute-start | bytes 245768 | tf_op jit(solution)/shard_map/ppermute | solution.py:27
  115.0 93.1 %collective-permute-start.6 = (f32[5,4096]{1,0:T(8,128)S(1)}, f32[5,4096]{1,0:T(8,128)S(1)}, u32[]{:S(2)}, u32[]{:S(2)}) collective-permute-start(f32[5,4096]{1,0:T(8,128)S(1)} %add.335), channel_id=1, source_target_pairs={{0,1},{1,0},{2,3},{3,2},{4,5},{5,4},{6,7},{7,6},{8,9},{9,8},{10,11... | collective-permute-start | bytes 245768 | tf_op jit(solution)/shard_map/ppermute | solution.py:32
  208.1 20.6 %collective-permute-start.7 = (f32[5,4096]{1,0:T(8,128)S(1)}, f32[5,4096]{1,0:T(8,128)S(1)}, u32[]{:S(2)}, u32[]{:S(2)}) collective-permute-start(f32[5,4096]{1,0:T(8,128)S(1)} %add.336), channel_id=1, source_target_pairs={{0,2},{1,3},{2,0},{3,1},{4,6},{5,7},{6,4},{7,5},{8,10},{9,11},{10,... | collective-permute-start | bytes 245768 | tf_op jit(solution)/shard_map/ppermute | solution.py:32

commit v2 on v1

v2 whole, which is shorter than its diff:
```python
import functools
import math

import jax
import jax.numpy as jnp
from jax import lax
from jax.experimental import pallas as pl
from jax.experimental.pallas import tpu as pltpu
from jax.sharding import PartitionSpec as P

LEAF = 128
CAND = 5

GAMMA = 5.0 / 3.0
SUPPORT = 1.5
KERNEL_NORM = 21.0 / (2.0 * math.pi * SUPPORT**3)
MOMENT_REG = 0.05
AREA_FLOOR = 0.0001
AWAY = 64.0
UNROLL = 8
ROWS = 64
F32 = jnp.float32
BF16 = jnp.bfloat16


def shifted(shard, axis, by):
    peers = lax.axis_size(axis)
    return lax.ppermute(shard, axis, [(i, (i + by) % peers) for i in range(peers)])


def swapped(shard, axis, mask):
    peers = lax.axis_size(axis)
    return lax.ppermute(shard, axis, [(i, i ^ mask) for i in range(peers)])


def reciprocal(value):
    return pl.reciprocal(value, approx=True)


def smoothing_of(dist_sq, scale):
    safe = jnp.maximum(dist_sq, 1e-12)
    radius = safe * lax.rsqrt(safe)
    inside = jnp.maximum(1.0 - radius * (1.0 / SUPPORT), 0.0)
    square = inside * inside
    return (square * square) * (scale + (scale * (4.0 / SUPPORT)) * radius)


def split_three(value):
    high = value.astype(BF16).astype(F32)
    rest = value - high
    middle = rest.astype(BF16).astype(F32)
    return high, middle, rest - middle


def stack_near(rows):
    high, middle, low = split_three(rows)
    return jnp.concatenate([high, high, high, middle, middle, low], axis=0).astype(BF16)


def stack_far(rows):
    high, middle, low = split_three(rows)
    return jnp.concatenate([high, middle, low, high, middle, high], axis=0).astype(BF16)


def bilinear(near_rows, far_rows):
    return lax.dot_general(
        stack_near(near_rows),
        stack_far(far_rows),
        (((0,), (0,)), ((), ())),
        preferred_element_type=F32,
    )


def moment_features(tile):
    row = lax.broadcasted_iota(jnp.int32, tile.shape, 0)
    by_x = tile * tile[0:1]
    by_y = jnp.where(row == 0, 1.0, tile * tile[1:2])
    by_z = tile * tile[2:3]
    whole = jnp.concatenate([tile, by_x, by_y, by_z], axis=0)
    high = whole.astype(BF16)
    low = (whole - high.astype(F32)).astype(BF16)
    both = jnp.concatenate([high, low], axis=0)
    return jnp.concatenate([both, both], axis=1)


def displacement(step_x, step_y, wrap):
    row = lax.broadcasted_iota(jnp.int32, (8, LEAF), 0)
    zero = jnp.zeros((8, LEAF), F32)
    out = jnp.where(row == 0, step_x, zero)
    out = jnp.where(row == 1, step_y, out)
    return jnp.where(row == 4, -wrap, out)


def finish_leaf(raw, tile):
    pos = [tile[k : k + 1] for k in range(3)]
    live = pos[0] < 0.5 * AWAY
    total = raw[16:17]
    first = [raw[k : k + 1] - pos[k] * total for k in range(3)]

    def second(left, right):
        lead = raw[8 + 8 * left + right : 9 + 8 * left + right]
        return lead - pos[left] * raw[right : right + 1] - pos[right] * first[left]

    density = jnp.where(live, total, 1.0)
    inverse_density = 1.0 / density

    def scaled(value):
        return jnp.where(live, value * inverse_density, 0.0)

    exx = scaled(second(0, 0)) + MOMENT_REG
    exy = scaled(second(0, 1))
    exz = scaled(second(0, 2))
    eyy = scaled(second(1, 1)) + MOMENT_REG
    eyz = scaled(second(1, 2))
    ezz = scaled(second(2, 2)) + MOMENT_REG
    mxx = eyy * ezz - eyz * eyz
    mxy = exz * eyz - exy * ezz
    mxz = exy * eyz - exz * eyy
    myy = exx * ezz - exz * exz
    myz = exy * exz - exx * eyz
    mzz = exx * eyy - exy * exy
    scale = 1.0 / (exx * mxx + exy * mxy + exz * mxz)
    inverse = [entry * scale for entry in (mxx, mxy, mxz, myy, myz, mzz)]
    square = inverse_density * inverse_density
    rows = [density] + [entry * square for entry in inverse]
    for quantity in range(3, 8):
        value = tile[quantity : quantity + 1]
        along = [
            scaled(
                raw[8 + 8 * k + quantity : 9 + 8 * k + quantity]
                - pos[k] * raw[quantity : quantity + 1]
                - value * first[k]
            )
            for k in range(3)
        ]
        half = [0.5 * term for term in along]
        rows.append(inverse[0] * half[0] + inverse[1] * half[1] + inverse[2] * half[2])
        rows.append(inverse[1] * half[0] + inverse[3] * half[1] + inverse[4] * half[2])
        rows.append(inverse[2] * half[0] + inverse[4] * half[1] + inverse[5] * half[2])
    rows.append(jnp.zeros((2, LEAF), F32))
    return jnp.concatenate(rows, axis=0)


def dot3(left, right):
    return left[0] * right[0] + left[1] * right[1] + left[2] * right[2]


def apply_sym(matrix, vector):
    return [
        dot3((matrix[0], matrix[1], matrix[2]), vector),
        dot3((matrix[1], matrix[3], matrix[4]), vector),
        dot3((matrix[2], matrix[4], matrix[5]), vector),
    ]


def stack_rows(rows):
    row = lax.broadcasted_iota(jnp.int32, (8, LEAF), 0)
    out = jnp.zeros((8, LEAF), F32)
    for k, entry in rows.items():
        out = jnp.where(row == k, entry, out)
    return out


def near_coefficients(tile, pay):
    pos = [tile[k : k + 1] for k in range(3)]
    out = [
        {0: dot3(pos, pos), 1: -2.0 * pos[0], 2: -2.0 * pos[1], 3: -2.0 * pos[2], 7: 1.0}
    ]
    matrix = [pay[1 + k : 2 + k] for k in range(6)]
    for line in ((0, 1, 2), (1, 3, 4), (2, 4, 5)):
        entries = [matrix[k] for k in line]
        out.append({0: -dot3(entries, pos), 1: entries[0], 2: entries[1], 3: entries[2]})
    for quantity in range(5):
        slope = [pay[7 + 3 * quantity + k : 8 + 3 * quantity + k] for k in range(3)]
        value = tile[3 + quantity : 4 + quantity]
        if quantity < 3:
            entry = {0: 0.5 * value - dot3(slope, pos), 4 + quantity: -0.5}
        else:
            entry = {0: value - dot3(slope, pos)}
        entry.update({1: slope[0], 2: slope[1], 3: slope[2]})
        out.append(entry)
    return [stack_rows(entry) for entry in out]


def far_coefficients(tile, pay):
    pos = [tile[k : k + 1] for k in range(3)]
    out = []
    matrix = [pay[1 + k : 2 + k] for k in range(6)]
    for line in ((0, 1, 2), (1, 3, 4), (2, 4, 5)):
        entries = [matrix[k] for k in line]
        out.append({0: dot3(entries, pos), 1: -entries[0], 2: -entries[1], 3: -entries[2]})
    for quantity in range(5):
        slope = [pay[7 + 3 * quantity + k : 8 + 3 * quantity + k] for k in range(3)]
        value = tile[3 + quantity : 4 + quantity]
        if quantity < 3:
            entry = {0: 0.5 * value - dot3(slope, pos), 4 + quantity: -0.5}
        else:
            entry = {0: value - dot3(slope, pos)}
        entry.update({1: slope[0], 2: slope[1], 3: slope[2]})
        out.append(entry)
    return [stack_rows(entry) for entry in out]


def shared_coefficients(tile):
    vel = [tile[3 + k : 4 + k] for k in range(3)]
    out = [{0: 0.5 * vel[k], 1 + k: -0.5} for k in range(3)]
    out += [{0: 0.5 * vel[k], 1 + k: 0.5} for k in range(3)]
    out += [{4: 1.0}, {5: 1.0}]
    out.append(
        {0: 0.125 * dot3(vel, vel), 1: 0.25 * vel[0], 2: 0.25 * vel[1], 3: 0.25 * vel[2], 6: 0.125}
    )
    return [stack_rows(entry) for entry in out]


def limited(value, low, high):
    return jnp.minimum(jnp.maximum(value, low), high)


def face_fluxes(near_out, far_out, shared_out, far_rho, far_press, weight):
    smooth = smoothing_of(near_out[0], KERNEL_NORM)
    toward = [near_out[1 + k] + far_out[k] for k in range(3)]
    length_sq = jnp.maximum(dot3(toward, toward), 1e-30)
    inverse_length = lax.rsqrt(length_sq)
    magnitude = smooth * (length_sq * inverse_length)
    scale = jnp.minimum(inverse_length, smooth * (1.0 / AREA_FLOOR))
    normal = [entry * scale for entry in toward]
    left_vel, right_vel = [], []
    for k in range(3):
        high = jnp.abs(shared_out[k])
        low = -high
        left_vel.append(limited(near_out[4 + k], low, high))
        right_vel.append(limited(far_out[3 + k], low, high))
    face_vel = shared_out[3:6]
    half_sq = shared_out[8]
    thermo = []
    for k, far_value in ((0, far_rho), (1, far_press)):
        low = jnp.minimum(shared_out[6 + k], far_value)
        high = jnp.maximum(shared_out[6 + k], far_value)
        thermo.append(limited(near_out[7 + k], low, high))
        thermo.append(limited(far_out[6 + k], low, high))
    left_rho, right_rho, left_p, right_p = thermo
    left_u = dot3(left_vel, normal)
    right_u = dot3(right_vel, normal)
    left_gp = GAMMA * left_p
    right_gp = GAMMA * right_p
    left_c = left_gp * lax.rsqrt(left_gp * left_rho)
    right_c = right_gp * lax.rsqrt(right_gp * right_rho)
    slow = jnp.minimum(left_u - left_c, right_u - right_c)
    fast = jnp.maximum(left_u + left_c, right_u + right_c)
    left_m = left_rho * (slow - left_u)
    right_m = right_rho * (fast - right_u)
    contact = (right_p - left_p + left_m * left_u - right_m * right_u) * reciprocal(
        left_m - right_m
    )
    is_left = contact >= 0.0
    speed = jnp.where(is_left, jnp.minimum(slow, 0.0), jnp.maximum(fast, 0.0))
    rho = jnp.where(is_left, left_rho, right_rho)
    press = jnp.where(is_left, left_p, right_p)
    normal_speed = jnp.where(is_left, left_u, right_u)
    vel = [jnp.where(is_left, left_vel[k], right_vel[k]) for k in range(3)]
    lag = speed - normal_speed
    ratio = lag * reciprocal(speed - contact)
    through = ratio * contact
    gain = speed * ratio - speed
    push = (rho * lag) * gain
    area = magnitude * weight
    mass = (rho * through) * area
    total_p = (press + push) * area
    mom = [mass * vel[k] + total_p * normal[k] for k in range(3)]
    energy = (press * (through * (1.0 / (GAMMA - 1.0)) + normal_speed + gain) + push * contact) * area
    energy = energy + (0.5 * dot3(vel, vel)) * mass
    energy = energy + dot3(face_vel, mom) + half_sq * mass
    return [mass] + [mom[k] + face_vel[k] * mass for k in range(3)] + [energy]


def pack_kernel(
    width,
    slab_ref,
    counts,
    positions,
    velocity,
    density,
    pressure,
    pair_list,
    packed,
):
    centre_x = slab_ref[0].astype(F32) + 0.5
    row = lax.broadcasted_iota(jnp.int32, (3, LEAF), 0)
    lane = lax.broadcasted_iota(jnp.int32, (3, LEAF), 1)

    def one_leaf(column, carry):
        lanes = pl.ds(pl.multiple_of(column * LEAF, LEAF), LEAF)
        centre_y = column.astype(F32) + 0.5
        centre = jnp.where(row == 0, centre_x, jnp.where(row == 1, centre_y, 0.5))
        dead = (row == 0) & (lane >= counts[column])
        packed[0:3, lanes] = jnp.where(dead, AWAY, positions[:, lanes] - centre)
        packed[3:6, lanes] = velocity[:, lanes]
        packed[6:7, lanes] = density[:, lanes]
        packed[7:8, lanes] = pressure[:, lanes]
        return carry

    lax.fori_loop(0, width, one_leaf, 0, unroll=4)
    particles = width * LEAF
    spare = packed.shape[1] - particles
    packed[:, particles:] = jnp.zeros((8, spare), F32)
    packed[0:3, particles : particles + pair_list.shape[1]] = pair_list[...].astype(F32)


def step_kernel(
    width,
    leaf_sub,
    slot_count,
    own_first,
    own_slots,
    rec,
    info,
    lower_ref,
    own_ref,
    upper_ref,
    beyond_ref,
    own_out,
    next_out,
    order,
    items,
    local,
    raw,
    pay,
    far_coef,
    near_left,
    far_left,
    shared_left,
    near_right,
    far_right,
    shared_right,
    dist,
    near_form,
    far_form,
    shared_form,
    col_sum,
    row_sum,
    row_rate,
):
    whole = 4 * width

    def load_leaf(column, carry):
        lanes = pl.ds(pl.multiple_of(column * LEAF, LEAF), LEAF)
        local[column] = lower_ref[:, lanes]
        local[width + column] = own_ref[:, lanes]
        local[2 * width + column] = upper_ref[:, lanes]
        local[3 * width + column] = beyond_ref[:, lanes]
        own_out[:, lanes] = jnp.zeros((5, LEAF), F32)
        next_out[:, lanes] = jnp.zeros((5, LEAF), F32)
        for slab in range(4):
            raw[slab * width + column] = jnp.zeros((32, LEAF), F32)
        return carry

    lax.fori_loop(0, width, load_leaf, 0)
    local[whole] = jnp.zeros((8, LEAF), F32)
    raw[whole] = jnp.zeros((32, LEAF), F32)

    def clear_rows(home, carry):
        for k in range(5):
            row_sum[home, k] = jnp.zeros((LEAF, LEAF), F32)
        return carry

    lax.fori_loop(0, leaf_sub, clear_rows, 0)

    def clear_cols(seat, carry):
        col_sum[seat] = jnp.zeros((40, LEAF), F32)
        return carry

    lax.fori_loop(0, 2 * leaf_sub + 3, clear_cols, 0)

    def collect(slot, used):
        order[used] = slot
        return used + rec[5, slot]

    used = lax.fori_loop(0, slot_count, collect, 0, unroll=8)
    for extra in range(2 * UNROLL):
        order[used + extra] = slot_count

    def slot_tiles(slot):
        shift = displacement(
            rec[2, slot].astype(F32), rec[3, slot].astype(F32), rec[4, slot].astype(F32)
        )
        return local[rec[0, slot]], local[rec[1, slot]] + shift, shift

    def distances(group):
        row = lax.broadcasted_iota(jnp.int32, (8, LEAF), 0)
        for k in range(UNROLL):
            near, far, _ = slot_tiles(order[group * UNROLL + k])
            near_pos = [near[j : j + 1] for j in range(3)]
            far_pos = [far[j : j + 1] for j in range(3)]
            near_k = jnp.where(
                row < 3,
                near,
                jnp.where(row == 3, dot3(near_pos, near_pos), jnp.where(row == 4, 1.0, 0.0)),
            )
            far_k = jnp.where(
                row < 3,
                -2.0 * far,
                jnp.where(row == 4, dot3(far_pos, far_pos), jnp.where(row == 3, 1.0, 0.0)),
            )
            dist[k] = bilinear(near_k, far_k)

    def moment_group(group, carry):
        parts = []
        for k in range(UNROLL):
            slot = order[group * UNROLL + k]
            near, far, shift = slot_tiles(slot)
            home = rec[0, slot]
            other = rec[1, slot]
            weight = jnp.where(home == other, 0.5, 1.0).astype(F32)
            smooth = smoothing_of(dist[k], KERNEL_NORM * weight)
            high = smooth.astype(BF16)
            low = (smooth - high.astype(F32)).astype(BF16)
            row_part = lax.dot_general(
                moment_features(far),
                jnp.concatenate([high, low], axis=1),
                (((1,), (1,)), ((), ())),
                preferred_element_type=F32,
            )
            col_part = lax.dot_general(
                moment_features(near - shift),
                jnp.concatenate([high, low], axis=0),
                (((1,), (0,)), ((), ())),
                preferred_element_type=F32,
            )
            parts.append((home, other, row_part, col_part))
        distances(group + 1)
        for home, other, row_part, col_part in parts:
            raw[home] += row_part[:32] + row_part[32:]
            raw[other] += col_part[:32] + col_part[32:]
        return carry

    distances(0)
    lax.fori_loop(0, (used + UNROLL - 1) // UNROLL, moment_group, 0)

    base = info[0]
    upper_base = info[1]

    def own_leaf(k):
        return width + lax.rem(base + k, width)

    def upper_leaf(k):
        return 2 * width + lax.rem(upper_base + k, width)

    def window_leaf(seat):
        return jnp.where(seat <= leaf_sub, own_leaf(seat), upper_leaf(seat - leaf_sub - 1))

    def finish(seat, carry):
        leaf = window_leaf(seat)
        payload = finish_leaf(raw[leaf], local[leaf])
        pay[seat] = payload
        for k, entry in enumerate(far_coefficients(local[leaf], payload)):
            far_coef[seat, 8 * k : 8 * k + 8] = entry
        return carry

    window = 2 * leaf_sub + 3
    lax.fori_loop(0, window, finish, 0)

    def turn_home(seat, carry):
        leaf = own_leaf(seat)
        tile = local[leaf]
        for k, entry in enumerate(near_coefficients(tile, pay[seat])):
            turned = stack_near(entry).T
            for part in range(LEAF // ROWS):
                near_left[seat, part, k * ROWS : (k + 1) * ROWS, 0:48] = turned[
                    part * ROWS : (part + 1) * ROWS
                ]
        vel = [tile[3 + k : 4 + k] for k in range(3)]
        generic = {0: 1.0}
        generic.update({1 + k: tile[k : k + 1] for k in range(6)})
        plain = {0: 1.0, 6: dot3(vel, vel)}
        plain.update({1 + k: tile[3 + k : 4 + k] for k in range(5)})
        far_left[seat, :, 0:48] = stack_near(stack_rows(generic)).T
        shared_left[seat, :, 0:48] = stack_near(stack_rows(plain)).T
        return carry

    lax.fori_loop(0, leaf_sub, turn_home, 0)

    def prepare_slot(index, count):
        slot = own_first + index
        other = rec[1, slot]
        other_seat = rec[7, slot]
        step_x = rec[2, slot].astype(F32)
        step_y = rec[3, slot].astype(F32)
        wrap = rec[4, slot].astype(F32)
        live = rec[6, slot]
        column = rec[0, slot] - width
        for part in range(LEAF // ROWS):
            items[count] = index * (LEAF // ROWS) + part
            filled = (info[8 + column] > part * ROWS).astype(jnp.int32)
            count = count + live * filled

        far = local[other] + displacement(step_x, step_y, wrap)
        row = lax.broadcasted_iota(jnp.int32, (8, LEAF), 0)
        pos = [far[k : k + 1] for k in range(3)]
        generic = {0: 1.0, 7: dot3(pos, pos)}
        generic.update({1 + k: far[k : k + 1] for k in range(6)})
        near_right[index] = stack_far(stack_rows(generic))
        for k in range(8):
            entry = far_coef[other_seat, 8 * k : 8 * k + 8]
            change = entry[1:2] * step_x + entry[2:3] * step_y
            if k == 4:
                change = change + 0.5 * wrap
            entry = jnp.where(row == 0, entry - change, entry)
            far_right[index, :, k * LEAF : (k + 1) * LEAF] = stack_far(entry)
        for k, entry in enumerate(shared_coefficients(far)):
            shared_right[index, :, k * LEAF : (k + 1) * LEAF] = stack_far(entry)
        return count

    item_count = lax.fori_loop(0, own_slots, prepare_slot, 0)
    items[item_count] = items[0]

    def forms(position):
        item = items[position]
        index = item // (LEAF // ROWS)
        part = item % (LEAF // ROWS)
        seat = rec[0, own_first + index] - width - base
        rows = pl.ds(pl.multiple_of(part * ROWS, ROWS), ROWS)
        near_form[...] = jnp.dot(
            near_left[seat, part, :, 0:48], near_right[index], preferred_element_type=F32
        )
        far_form[...] = jnp.dot(
            far_left[seat, rows, 0:48], far_right[index], preferred_element_type=F32
        )
        shared_form[...] = jnp.dot(
            shared_left[seat, rows, 0:48], shared_right[index], preferred_element_type=F32
        )

    def flux_item(position, carry):
        item = items[position]
        index = item // (LEAF // ROWS)
        part = item % (LEAF // ROWS)
        home = rec[0, own_first + index]
        other = rec[1, own_first + index]
        other_seat = rec[7, own_first + index]
        seat = home - width - base
        rows = pl.ds(pl.multiple_of(part * ROWS, ROWS), ROWS)
        weight = jnp.where(home == other, 0.5, 1.0).astype(F32)
        fluxes = face_fluxes(
            [near_form[k * ROWS : (k + 1) * ROWS, :] for k in range(9)],
            [far_form[:, k * LEAF : (k + 1) * LEAF] for k in range(8)],
            [shared_form[:, k * LEAF : (k + 1) * LEAF] for k in range(9)],
            local[other, 6:7, :],
            local[other, 7:8, :],
            weight,
        )
        forms(position + 1)
        for k in range(5):
            row_sum[seat, k, rows, :] += fluxes[k]
            col_sum[other_seat, 8 * k : 8 * k + 8] += sum(
                fluxes[k][8 * j : 8 * j + 8] for j in range(ROWS // 8)
            )
        return carry

    forms(0)
    lax.fori_loop(0, item_count, flux_item, 0)

    lane = lax.broadcasted_iota(jnp.int32, (LEAF, LEAF), 1)

    def row_total(seat, carry):
        total = jnp.zeros((LEAF, LEAF), F32)
        for c in range(5):
            total = jnp.where(lane == c, jnp.sum(row_sum[seat, c], axis=1, keepdims=True), total)
        row_rate[seat] = total.T[0:8]
        return carry

    lax.fori_loop(0, leaf_sub, row_total, 0)
    row_rate[leaf_sub] = jnp.zeros((8, LEAF), F32)

    def rates(seat, less):
        leaf = window_leaf(seat)
        total = stack_rows(
            {
                k: jnp.sum(col_sum[seat, 8 * k : 8 * k + 8], axis=0, keepdims=True)
                for k in range(5)
            }
        )
        if less is not None:
            total = total - less
        live = local[leaf][0:1] < 0.5 * AWAY
        column = lax.rem(leaf, width)
        lanes = pl.ds(pl.multiple_of(column * LEAF, LEAF), LEAF)
        return lanes, jnp.where(live, total * pay[seat][0:1], 0.0)[0:5]

    def write_own(k, carry):
        lanes, value = rates(k, row_rate[k])
        own_out[:, lanes] = value
        return carry

    def write_upper(k, carry):
        lanes, value = rates(k, None)
        next_out[:, lanes] = value
        return carry

    lax.fori_loop(0, leaf_sub + 1, write_own, 0)
    lax.fori_loop(leaf_sub + 1, window, write_upper, 0)


def shards(positions, velocity, density, pressure, counts, pair_list):
    width = counts.shape[0]
    slots = pair_list.shape[1]
    particles = width * LEAF
    sub_count = lax.axis_size("sub")
    leaf_sub = width // sub_count
    slab_index = lax.axis_index("slab")
    sub_index = lax.axis_index("sub")

    smem = pl.BlockSpec(memory_space=pltpu.SMEM)
    vmem = pl.BlockSpec(memory_space=pltpu.VMEM)
    lanes = -(-slots // LEAF) * LEAF
    packed = pl.pallas_call(
        functools.partial(pack_kernel, width),
        out_shape=jax.ShapeDtypeStruct((8, particles + lanes), F32),
        in_specs=[smem, smem, vmem, vmem, vmem, vmem, vmem],
        out_specs=vmem,
        name="pack",
    )(
        slab_index.astype(jnp.int32).reshape(1),
        counts,
        positions,
        velocity,
        density[None],
        pressure[None],
        pair_list,
    )
    lower = shifted(packed, "slab", 1)
    upper = shifted(packed, "slab", -1)
    beyond = shifted(packed, "slab", -2)

    lists = jnp.stack(
        [entry[0:3, particles : particles + slots] for entry in (lower, packed, upper)]
    )[None]
    mask = 1
    while mask < sub_count:
        lists = jnp.concatenate([lists, swapped(lists, "sub", mask)], axis=0)
        mask *= 2
    lists = lists.astype(jnp.int32)
    head, tail, offset = lists[:, :, 0], lists[:, :, 1], lists[:, :, 2]
    occupied = head >= 0
    head = jnp.where(occupied, head, 0)
    tail = jnp.where(occupied, tail, 0)
    head_col, tail_col = head % width, tail % width
    step_x = (head // width != tail // width).astype(jnp.int32)
    wrap = (tail // width < head // width).astype(jnp.int32)
    from_slab = jnp.arange(3, dtype=jnp.int32)[None, :, None]
    home = from_slab * width + head_col
    other = (from_slab + step_x) * width + tail_col
    step_y = tail_col + offset - head_col
    own_shift = jnp.max(
        jnp.where(occupied[0, 1] & (step_x[0, 1] > 0), (-offset[0, 1]) % width, 0)
    )
    base = sub_index * leaf_sub
    upper_base = (base - 1 + own_shift) % width

    def wanted(leaf_slab, leaf_column):
        in_own = (leaf_slab == 1) & ((leaf_column - base) % width <= leaf_sub)
        in_upper = (leaf_slab == 2) & ((leaf_column - upper_base) % width <= leaf_sub + 1)
        return in_own | in_upper

    needed = occupied & (wanted(from_slab, head_col) | wanted(from_slab + step_x, tail_col))
    other_seat = jnp.where(
        step_x > 0,
        jnp.minimum((tail_col - upper_base) % width, leaf_sub + 1) + leaf_sub + 1,
        jnp.minimum((tail_col - base) % width, leaf_sub),
    )
    slot_count = sub_count * 3 * slots
    own_items = slots * (LEAF // ROWS) + 1
    rec = jnp.stack(
        [
            jnp.broadcast_to(entry, head.shape).reshape(-1)
            for entry in (
                home,
                other,
                step_x,
                step_y,
                wrap,
                needed.astype(jnp.int32),
                occupied.astype(jnp.int32),
                other_seat,
            )
        ]
    )
    spare = jnp.array([[4 * width], [4 * width], [0], [0], [0], [0], [0], [0]], jnp.int32)
    rec = jnp.concatenate([rec, spare], axis=1)
    info = jnp.concatenate(
        [base[None], upper_base[None], jnp.zeros((6,), jnp.int32), counts]
    ).astype(jnp.int32)

    own_part, next_part = pl.pallas_call(
        functools.partial(step_kernel, width, leaf_sub, slot_count, slots, slots),
        out_shape=[jax.ShapeDtypeStruct((5, particles), F32)] * 2,
        in_specs=[smem, smem, vmem, vmem, vmem, vmem],
        out_specs=[vmem, vmem],
        scratch_shapes=[
            pltpu.SMEM((slot_count + 2 * UNROLL,), jnp.int32),
            pltpu.SMEM((own_items,), jnp.int32),
            pltpu.VMEM((4 * width + 1, 8, LEAF), F32),
            pltpu.VMEM((4 * width + 1, 32, LEAF), F32),
            pltpu.VMEM((2 * leaf_sub + 3, 24, LEAF), F32),
            pltpu.VMEM((2 * leaf_sub + 3, 64, LEAF), F32),
            pltpu.VMEM((leaf_sub, LEAF // ROWS, 9 * ROWS, LEAF), BF16),
            pltpu.VMEM((leaf_sub, LEAF, LEAF), BF16),
            pltpu.VMEM((leaf_sub, LEAF, LEAF), BF16),
            pltpu.VMEM((slots, 48, LEAF), BF16),
            pltpu.VMEM((slots, 48, 8 * LEAF), BF16),
            pltpu.VMEM((slots, 48, 9 * LEAF), BF16),
            pltpu.VMEM((UNROLL, LEAF, LEAF), F32),
            pltpu.VMEM((9 * ROWS, LEAF), F32),
            pltpu.VMEM((ROWS, 8 * LEAF), F32),
            pltpu.VMEM((ROWS, 9 * LEAF), F32),
            pltpu.VMEM((2 * leaf_sub + 3, 40, LEAF), F32),
            pltpu.VMEM((leaf_sub, 5, LEAF, LEAF), F32),
            pltpu.VMEM((leaf_sub + 1, 8, LEAF), F32),
        ],
        compiler_params=pltpu.CompilerParams(vmem_limit_bytes=48 * 1024 * 1024),
        name="hydro_step",
    )(rec, info, lower, packed, upper, beyond)

    merged = own_part + shifted(next_part, "slab", 1)
    mask = 1
    while mask < sub_count:
        merged = merged + swapped(merged, "sub", mask)
        mask *= 2
    return merged


def solution(mesh):
    placed = (
        P(None, "slab"),
        P(None, "slab"),
        P("slab"),
        P("slab"),
        P("slab"),
        P(None, ("slab", "sub")),
    )
    return jax.shard_map(
        shards, mesh=mesh, in_specs=placed, out_specs=P(None, "slab"), check_vma=False
    )
```

time: 234 us -> 84.8 us (0.36)
  the two profiles are of different devices: /device:TPU:2 before, /device:TPU:0 now
where the time goes in v2:
time: 84.8 us; the launch traced here: 85.4 us
  Pallas kernels  43.5 us (51%)
  waiting for transfers between devices  22.4 us (26%)
  starting transfers between devices  14.1 us (17%)
  local copies, waits for them, and re-layouts  2.85 us (3%)
  other arithmetic  1.79 us (2%)
  between operations  0.86 us (1%)
    pallas_call x1, Pallas kernels, shards(): pl.pallas_call(functools.partial(step_kernel, width, leaf_sub, slot_count...  41.7 us
    ppermute x4, waiting for transfers between devices, swapped(): return lax.ppermute(shard, axis, [(i, i ^ mask) for i in range(peers)])  11.3 us
    ppermute x4, waiting for transfers between devices, shifted(): lax.ppermute(shard, axis, [(i, (i + by) % peers) for i in range(peers)])  11 us
    ppermute x4, starting transfers between devices, swapped(): return lax.ppermute(shard, axis, [(i, i ^ mask) for i in range(peers)])  9.6 us
    ppermute x4, starting transfers between devices, shifted(): lax.ppermute(shard, axis, [(i, (i + by) % peers) for i in range(peers)])  4.46 us
    pallas_call x1, Pallas kernels, shards(): pl.pallas_call(functools.partial(pack_kernel, width), out_shape=jax.Shape...  1.71 us
  transfers between devices with their start and end apart: 8, of which 7 were waited for; matrix products, arithmetic and copies ran while one was open for 3% of the time, Pallas kernels for 0%

profile of v2, /device:TPU:0, one launch (start us, length us, event | category | flops | bytes accessed | tf_op | source)
XLA Modules:
  0.0 85.4 jit_solution(14894413974234320029)
XLA Ops:
  0.0 1.7 %pack.1.own_ref = f32[8,4224]{1,0:T(8,128)} custom-call(s32[1]{0:T(128)} %bitcast.slab_ref, s32[32]{0:T(128)} %counts.1, f32[3,4096]{1,0:T(4,128)} %positions.1, f32[3,4096]{1,0:T(4,128)} %velocity.1, f32[1,4096]{1,0:T(1,128)} %bitcast.36, f32[1,4096]{1,0:T(1,128)} %bitcast.37, s32[3,40]{1,0:T(4,128)} %pair_list.1), custom_call_target="tpu_custom_call" | custom-call | tf_op jit(solution)/shard_map/pack/pallas_call | solution.py:614
  1.7 3.9 %collective-permute-start.4 = (f32[8,4224]{1,0:T(8,128)}, f32[8,4224]{1,0:T(8,128)S(1)}, u32[]{:S(2)}, u32[]{:S(2)}) collective-permute-start(f32[8,4224]{1,0:T(8,128)} %pack.1.own_ref), channel_id=1, source_target_pairs={{0,24},{4,28},{8,0},{12,4},{16,8},{20,12},{24,16},{28,20},{1,25},{... | collective-permute-start | bytes 405512 | tf_op jit(solution)/shard_map/ppermute | solution.py:28
  5.6 0.0 collective-permute-start.1
  5.6 0.5 collective-permute-start
  6.1 0.7 slice_bitcast_fusion.1
  6.8 4.9 %collective-permute-done.1.upper_ref = f32[8,4224]{1,0:T(8,128)S(1)} collective-permute-done((f32[8,4224]{1,0:T(8,128)}, f32[8,4224]{1,0:T(8,128)S(1)}, u32[]{:S(2)}, u32[]{:S(2)}) %collective-permute-start.1) | collective-permute-done | bytes 135200 | tf_op jit(solution)/shard_map/ppermute | solution.py:28
  11.7 0.9 %collective-permute-done.lower_ref = f32[8,4224]{1,0:T(8,128)S(1)} collective-permute-done((f32[8,4224]{1,0:T(8,128)}, f32[8,4224]{1,0:T(8,128)S(1)}, u32[]{:S(2)}, u32[]{:S(2)}) %collective-permute-start) | collective-permute-done | bytes 135200 | tf_op jit(solution)/shard_map/ppermute | solution.py:28
  12.6 1.6 %collective-permute-start.2 = (f32[1,3,3,40]{3,2,1,0:T(4,128)S(1)}, f32[1,3,3,40]{3,2,1,0:T(4,128)S(1)}, u32[]{:S(2)}, u32[]{:S(2)}) collective-permute-start(f32[1,3,3,40]{3,2,1,0:T(4,128)S(1)} %maximum_bitcast_fusion), channel_id=1, source_target_pairs={{0,1},{1,0},{2,3},{3,2},{4,5},{5,4},{6,7},{7,6},{8,9},{9,8},{10,11... | collective-permute-start | bytes 4328 | tf_op jit(solution)/shard_map/ppermute | solution.py:33
  14.2 2.0 %collective-permute-done.2 = f32[1,3,3,40]{3,2,1,0:T(4,128)S(1)} collective-permute-done((f32[1,3,3,40]{3,2,1,0:T(4,128)S(1)}, f32[1,3,3,40]{3,2,1,0:T(4,128)S(1)}, u32[]{:S(2)}, u32[]{:S(2)}) %collective-permute-start.2) | collective-permute-done | bytes 1472 | tf_op jit(solution)/shard_map/ppermute | solution.py:33
  16.3 2.6 %collective-permute-start.3 = (f32[2,3,3,40]{3,2,1,0:T(4,128)S(1)}, f32[2,3,3,40]{3,2,1,0:T(4,128)S(1)}, u32[]{:S(2)}, u32[]{:S(2)}) collective-permute-start(f32[2,3,3,40]{3,2,1,0:T(4,128)S(1)} %pad_maximum_fusion), channel_id=1, source_target_pairs={{0,2},{1,3},{2,0},{3,1},{4,6},{5,7},{6,4},{7,5},{8,10},{9,11},{10,... | collective-permute-start | bytes 8648 | tf_op jit(solution)/shard_map/ppermute | solution.py:33
  18.9 0.1 and.339
  18.9 0.1 and.340
  19.0 0.1 and.335
  19.1 0.1 and.336
  19.2 0.1 add.246
  19.3 0.1 add.247
  19.4 0.1 add.251
  19.5 1.4 %collective-permute-done.3 = f32[2,3,3,40]{3,2,1,0:T(4,128)S(1)} collective-permute-done((f32[2,3,3,40]{3,2,1,0:T(4,128)S(1)}, f32[2,3,3,40]{3,2,1,0:T(4,128)S(1)}, u32[]{:S(2)}, u32[]{:S(2)}) %collective-permute-start.3) | collective-permute-done | bytes 2912 | tf_op jit(solution)/shard_map/ppermute | solution.py:33
  20.9 0.1 fusion.13
  21.0 0.0 copy-start
  21.0 0.7 fusion.9
  22.3 0.1 squeeze.21
  22.4 0.1 squeeze.20
  22.5 0.1 squeeze.22
  22.6 0.1 compare_select_fusion.8
  22.7 0.1 fusion.7
  22.8 0.0 copy-start.2
  22.8 0.6 copy-done.2
  23.4 0.1 pad_add_fusion.1.info
  23.5 0.0 copy-start.1
  23.6 0.6 copy-done.1
  24.2 0.1 pad_add_fusion.rec
  24.3 0.0 collective-permute-done.4.beyond_ref
  24.3 0.0 copy-done
  24.3 41.7 %hydro_step.1 = (f32[5,4096]{1,0:T(8,128)S(1)}, f32[5,4096]{1,0:T(8,128)S(1)}) custom-call(s32[8,481]{1,0:T(8,128)S(1)} %pad_add_fusion.rec, s32[40]{0:T(128)S(1)} %pad_add_fusion.1.info, f32[8,4224]{1,0:T(8,128)S(1)} %collective-permute-done.lower_ref, f32[8,4224]{1,0:T(8,128)S(1)} %copy-done, f32[8,4224]{1,0:T(8,128)S(1)} %collective-permute-done.1.upper_ref, ...), custom_call_target="tpu_custom_call" | custom-call | tf_op jit(solution)/shard_map/hydro_step/pallas_call | solution.py:692
  66.0 0.1 collective-permute-start.5
  66.1 5.3 %collective-permute-done.5 = f32[5,4096]{1,0:T(8,128)S(1)} collective-permute-done((f32[5,4096]{1,0:T(8,128)S(1)}, f32[5,4096]{1,0:T(8,128)S(1)}, u32[]{:S(2)}, u32[]{:S(2)}) %collective-permute-start.5) | collective-permute-done | bytes 81952 | tf_op jit(solution)/shard_map/ppermute | solution.py:28
  71.4 0.1 collective-permute-start.6
  71.5 5.0 %collective-permute-done.6 = f32[5,4096]{1,0:T(8,128)S(1)} collective-permute-done((f32[5,4096]{1,0:T(8,128)S(1)}, f32[5,4096]{1,0:T(8,128)S(1)}, u32[]{:S(2)}, u32[]{:S(2)}) %collective-permute-start.6) | collective-permute-done | bytes 81952 | tf_op jit(solution)/shard_map/ppermute | solution.py:33
  76.4 5.3 %collective-permute-start.7 = (f32[5,4096]{1,0:T(8,128)S(1)}, f32[5,4096]{1,0:T(8,128)S(1)}, u32[]{:S(2)}, u32[]{:S(2)}) collective-permute-start(f32[5,4096]{1,0:T(8,128)S(1)} %add.265), channel_id=1, source_target_pairs={{0,2},{1,3},{2,0},{3,1},{4,6},{5,7},{6,4},{7,5},{8,10},{9,11},{10,... | collective-permute-start | bytes 245768 | tf_op jit(solution)/shard_map/ppermute | solution.py:33
  81.7 2.9 %collective-permute-done.7 = f32[5,4096]{1,0:T(8,128)S(1)} collective-permute-done((f32[5,4096]{1,0:T(8,128)S(1)}, f32[5,4096]{1,0:T(8,128)S(1)}, u32[]{:S(2)}, u32[]{:S(2)}) %collective-permute-start.7) | collective-permute-done | bytes 81952 | tf_op jit(solution)/shard_map/ppermute | solution.py:33
  84.7 0.7 add.266
  (18 shorter events, 0.2 us)
Async XLA Ops:
  1.7 22.6 %collective-permute-start.4 = (f32[8,4224]{1,0:T(8,128)}, f32[8,4224]{1,0:T(8,128)S(1)}, u32[]{:S(2)}, u32[]{:S(2)}) collective-permute-start(f32[8,4224]{1,0:T(8,128)} %pack.1.own_ref), channel_id=1, source_target_pairs={{0,24},{4,28},{8,0},{12,4},{16,8},{20,12},{24,16},{28,20},{1,25},{... | collective-permute-start | bytes 405512 | tf_op jit(solution)/shard_map/ppermute | solution.py:28
  5.6 6.1 %collective-permute-start.1 = (f32[8,4224]{1,0:T(8,128)}, f32[8,4224]{1,0:T(8,128)S(1)}, u32[]{:S(2)}, u32[]{:S(2)}) collective-permute-start(f32[8,4224]{1,0:T(8,128)} %pack.1.own_ref), channel_id=1, source_target_pairs={{0,28},{4,0},{8,4},{12,8},{16,12},{20,16},{24,20},{28,24},{1,29},{... | collective-permute-start | bytes 405512 | tf_op jit(solution)/shard_map/ppermute | solution.py:28
  5.6 6.9 %collective-permute-start = (f32[8,4224]{1,0:T(8,128)}, f32[8,4224]{1,0:T(8,128)S(1)}, u32[]{:S(2)}, u32[]{:S(2)}) collective-permute-start(f32[8,4224]{1,0:T(8,128)} %pack.1.own_ref), channel_id=1, source_target_pairs={{0,4},{4,8},{8,12},{12,16},{16,20},{20,24},{24,28},{28,0},{1,5},{5... | collective-permute-start | bytes 405512 | tf_op jit(solution)/shard_map/ppermute | solution.py:28
  12.6 3.7 %collective-permute-start.2 = (f32[1,3,3,40]{3,2,1,0:T(4,128)S(1)}, f32[1,3,3,40]{3,2,1,0:T(4,128)S(1)}, u32[]{:S(2)}, u32[]{:S(2)}) collective-permute-start(f32[1,3,3,40]{3,2,1,0:T(4,128)S(1)} %maximum_bitcast_fusion), channel_id=1, source_target_pairs={{0,1},{1,0},{2,3},{3,2},{4,5},{5,4},{6,7},{7,6},{8,9},{9,8},{10,11... | collective-permute-start | bytes 4328 | tf_op jit(solution)/shard_map/ppermute | solution.py:33
  16.3 4.6 %collective-permute-start.3 = (f32[2,3,3,40]{3,2,1,0:T(4,128)S(1)}, f32[2,3,3,40]{3,2,1,0:T(4,128)S(1)}, u32[]{:S(2)}, u32[]{:S(2)}) collective-permute-start(f32[2,3,3,40]{3,2,1,0:T(4,128)S(1)} %pad_maximum_fusion), channel_id=1, source_target_pairs={{0,2},{1,3},{2,0},{3,1},{4,6},{5,7},{6,4},{7,5},{8,10},{9,11},{10,... | collective-permute-start | bytes 8648 | tf_op jit(solution)/shard_map/ppermute | solution.py:33
  21.0 3.3 %copy-start = (f32[8,4224]{1,0:T(8,128)S(1)}, f32[8,4224]{1,0:T(8,128)}, u32[]{:S(2)}) copy-start(f32[8,4224]{1,0:T(8,128)} %pack.1.own_ref) | copy-start | bytes 405508
  22.8 0.7 copy-start.2
  23.5 0.7 copy-start.1
  66.0 5.3 %collective-permute-start.5 = (f32[5,4096]{1,0:T(8,128)S(1)}, f32[5,4096]{1,0:T(8,128)S(1)}, u32[]{:S(2)}, u32[]{:S(2)}) collective-permute-start(f32[5,4096]{1,0:T(8,128)S(1)} %get-tuple-element.8), channel_id=1, source_target_pairs={{0,4},{4,8},{8,12},{12,16},{16,20},{20,24},{24,28},{28,0},{1,5},{5... | collective-permute-start | bytes 245768 | tf_op jit(solution)/shard_map/ppermute | solution.py:28
  71.4 5.0 %collective-permute-start.6 = (f32[5,4096]{1,0:T(8,128)S(1)}, f32[5,4096]{1,0:T(8,128)S(1)}, u32[]{:S(2)}, u32[]{:S(2)}) collective-permute-start(f32[5,4096]{1,0:T(8,128)S(1)} %add.264), channel_id=1, source_target_pairs={{0,1},{1,0},{2,3},{3,2},{4,5},{5,4},{6,7},{7,6},{8,9},{9,8},{10,11... | collective-permute-start | bytes 245768 | tf_op jit(solution)/shard_map/ppermute | solution.py:33
  76.4 8.2 %collective-permute-start.7 = (f32[5,4096]{1,0:T(8,128)S(1)}, f32[5,4096]{1,0:T(8,128)S(1)}, u32[]{:S(2)}, u32[]{:S(2)}) collective-permute-start(f32[5,4096]{1,0:T(8,128)S(1)} %add.265), channel_id=1, source_target_pairs={{0,2},{1,3},{2,0},{3,1},{4,6},{5,7},{6,4},{7,5},{8,10},{9,11},{10,... | collective-permute-start | bytes 245768 | tf_op jit(solution)/shard_map/ppermute | solution.py:33
